TPU v7x, 256 devices: a whole 4x4x8 slice. The times are simulated.
256 devices in a mesh: tm: 8 (over y_hi, x), row: 32 (over y_lo, z, core).
Axes of the slice: x: 4, y: 4 (y_hi: 2, y_lo: 2; y = y_hi * 2 + y_lo), z: 8, core: 2. Of those that a mesh axis runs over, the one named last changes fastest.
Arguments:
- field: float32 [1, 2048, 16384], P(None, 'row', 'tm'), may hold values from -6 to 6
- screen: float32 [1, 2048], P(None, 'row'), may hold values from -1.8 to 1.8
Outputs:
- spectrum: float32 [2, 1, 8192, 2048], P(None, None, ('tm', 'row'))
All inputs are finite; a program needn't handle non-finite values.
Results may differ from a plain program's by a relative error of at most 0.00024.
Values sent between devices are 32-bit elements; how exact they have to be, the bound alone decides.
No kernel may reach another device: no remote copies, remote signals or barrier semaphores. Data moves between devices by JAX's collectives and lax.ppermute only.
A program may use at most 64 MiB of HBM per device.

v0:
```python
import math

import jax
import jax.numpy as jnp
from jax import lax
from jax.sharding import PartitionSpec as P

NX = 2048
NT = 16384
NF = 8192


kerr_coeff = 0.3
ionize_rate = 0.4
highest = lax.Precision.HIGHEST


def carried_in(value, axis, combine, identity):
    peers, mine = (lax.axis_size(axis), lax.axis_index(axis))
    everything = lax.all_gather(value, axis)
    start = jnp.broadcast_to(jnp.asarray(identity, value.dtype), value.shape)

    def lap(k, before):
        reached = k < mine
        new = combine(before, everything[k])
        return jnp.where(reached, new, before)

    return lax.fori_loop(0, peers, lap, start)


def source_weights(scaled):
    return (0.2 * scaled, 0.5 / (1.0 + 64.0 * scaled * scaled))


def phase_angle(scaled, transverse):
    return 40.0 * scaled * (1.0 + 0.3 * scaled * scaled) - 20.0 * transverse * transverse / (
        scaled + 0.05
    )


def dft_tables(height, breadth, period):
    left_index = jnp.arange(height, dtype=jnp.int32)[:, None]
    right_index = jnp.arange(breadth, dtype=jnp.int32)[None, :]
    turns = (left_index * right_index % period).astype(jnp.float32) * (2.0 * math.pi / period)
    return (jnp.cos(turns), jnp.sin(turns))


def running_sum(values):
    length = values.shape[-1]
    blocks = values.reshape(values.shape[:-1] + (length // 128, 128))
    triangle = (jnp.arange(128)[:, None] <= jnp.arange(128)[None, :]).astype(jnp.float32)
    within = jnp.einsum("...bi,ij->...bj", blocks, triangle, precision=highest)
    totals = within[..., -1]
    earlier = jnp.cumsum(totals, axis=-1) - totals
    return (within + earlier[..., None]).reshape(values.shape)


def nonlinear_terms(sample, screen_part, density):
    polarization = kerr_coeff * sample**3 + 2.0 * screen_part[..., None] * sample
    return (polarization, density * sample)


def combine_sum(earlier, following):
    return earlier + following


def time_spectrum(signal):
    rows_here, points, length = signal.shape
    inner = 128
    outer = length // inner
    grid = signal.reshape(rows_here, points, outer, inner)
    cos_one, sin_one = dft_tables(outer, outer, outer)
    first_re = jnp.einsum("rjab,ak->rjbk", grid, cos_one, precision=highest)
    first_im = -jnp.einsum("rjab,ak->rjbk", grid, sin_one, precision=highest)
    cos_twist, sin_twist = dft_tables(inner, outer, length)
    second_re = first_re * cos_twist + first_im * sin_twist
    second_im = first_im * cos_twist - first_re * sin_twist
    cos_two, sin_two = dft_tables(inner // 2, inner, inner)
    cos_wide = jnp.broadcast_to(cos_two, (rows_here, points, inner // 2, inner))
    sin_wide = jnp.broadcast_to(sin_two, (rows_here, points, inner // 2, inner))
    spec_re = jnp.matmul(cos_wide, second_re, precision=highest) + jnp.matmul(
        sin_wide, second_im, precision=highest
    )
    spec_im = jnp.matmul(cos_wide, second_im, precision=highest) - jnp.matmul(
        sin_wide, second_re, precision=highest
    )
    factor = 1.0 / math.sqrt(length)
    target = (rows_here, points, length // 2)
    return (spec_re.reshape(target) * factor, spec_im.reshape(target) * factor)


def per_device(field, screen):
    tm_count = lax.axis_size("tm")
    row_count = lax.axis_size("row")
    rows_here, local_x, local_t = field.shape
    points = local_x // tm_count
    running = running_sum(field**4)
    offset = carried_in(
        running[..., -1], "tm", combine_sum, jnp.zeros(running.shape[:-1], jnp.float32)
    )
    density = ionize_rate / NT * (running + offset[..., None])
    polarization, current = nonlinear_terms(field, screen, density)
    stacked = jnp.stack([field, polarization, current])
    signals = lax.all_to_all(stacked, "tm", split_axis=2, concat_axis=3, tiled=True)
    sample = signals[0]
    polarization = signals[1]
    current = signals[2]
    scaled = jnp.arange(NF, dtype=jnp.int32).astype(jnp.float32) / NF
    weight_kerr, weight_plasma = source_weights(scaled)
    base_re, base_im = time_spectrum(sample)
    kerr_re, kerr_im = time_spectrum(polarization)
    plasma_re, plasma_im = time_spectrum(current)
    mixed_re = base_re - weight_kerr * kerr_im - weight_plasma * plasma_re
    mixed_im = base_im + weight_kerr * kerr_re - weight_plasma * plasma_im
    block = NF // (tm_count * row_count)
    packed = jnp.stack([mixed_re, mixed_im]).reshape(
        2, rows_here, 1, 1, points, tm_count, row_count, block
    )
    moved = lax.all_to_all(
        lax.all_to_all(packed, "tm", split_axis=5, concat_axis=3, tiled=True),
        "row",
        split_axis=6,
        concat_axis=2,
        tiled=True,
    )
    moved = moved.reshape(2, rows_here, NX, block)
    real_part = moved[0]
    imag_part = moved[1]
    cos_full, sin_full = dft_tables(NX, NX, NX)
    final_re = jnp.einsum("rxf,xq->rfq", real_part, cos_full, precision=highest) + jnp.einsum(
        "rxf,xq->rfq", imag_part, sin_full, precision=highest
    )
    final_im = jnp.einsum("rxf,xq->rfq", imag_part, cos_full, precision=highest) - jnp.einsum(
        "rxf,xq->rfq", real_part, sin_full, precision=highest
    )
    factor = 1.0 / math.sqrt(NX)
    final_re = final_re * factor
    final_im = final_im * factor
    start = (lax.axis_index("tm") * row_count + lax.axis_index("row")) * block
    bin_here = (start + jnp.arange(block, dtype=jnp.int32)).astype(jnp.float32) / NF
    kx_index = jnp.arange(NX, dtype=jnp.int32)
    transverse = jnp.where(kx_index < NX // 2, kx_index, kx_index - NX).astype(jnp.float32) / (
        NX // 2
    )
    phase_table = phase_angle(bin_here[:, None], transverse[None, :])
    cos_phase = jnp.cos(phase_table)
    sin_phase = jnp.sin(phase_table)
    out_re = final_re * cos_phase - final_im * sin_phase
    out_im = final_re * sin_phase + final_im * cos_phase
    return jnp.stack([out_re, out_im])


def solution(mesh):
    return jax.shard_map(
        per_device,
        mesh=mesh,
        in_specs=(P(None, "row", "tm"), P(None, "row")),
        out_specs=P(None, None, ("tm", "row"), None),
        check_vma=False,
    )
```

profile of v0, /device:TPU:1, one launch (start us, length us, event | category | flops | bytes accessed | tf_op | source)
XLA Modules:
  0.0 459.8 jit_solution(9290329612982870312)
XLA Ops:
  7.9 20.4 %all-gather = f32[8,64,1]{1,2,0:T(1,128)S(1)} all-gather(f32[1,64,1]{1,2,0:T(1,128)S(1)} %slice.34), channel_id=2, replica_groups=mesh['tm'=8,'row'=32] {'tm'}, dimensions={0}, use_global_device_ids=true | all-gather | bytes 2304 | tf_op jit(solution)/shard_map/all_gather | solution.py:20
  28.6 1.6 fusion.34
  30.2 2.5 pad_maximum_fusion.1
  32.7 4.0 all-to-all-start
  38.0 21.1 %all-to-all-done = f32[3,1,64,2048]{3,1,0,2:T(1,128)S(1)} async-done(((f32[3,1,64,2048]{3,1,0,2:T(1,128)}), f32[3,1,64,2048]{3,1,0,2:T(1,128)S(1)}, u32[]{:S(2)}, u32[]{:S(2)}) %all-to-all-start) | async-done | bytes 1572896 | tf_op jit(solution)/shard_map/all_to_all | solution.py:104
  67.5 2.2 fusion.62
  78.3 2.2 mul.734
  80.5 2.3 convolution_add_fusion
  82.7 2.2 reshape.446
  85.0 2.3 convolution_subtract_fusion
  87.2 2.2 reshape.447
  89.4 2.3 convolution_subtract_fusion.2
  91.7 2.3 reshape.443
  97.7 8.8 %fusion.31 = (f32[1,1,1,1,8,8,32,32]{7,4,6,0,3,2,1,5:T(8,128)S(1)}, f32[1,1,1,1,8,8,32,32]{7,4,6,0,3,2,1,5:T(8,128)S(1)}) fusion(f32[1,1,1,1,8,8,32,32]{7,6,5,4,3,2,1,0:T(8,128)S(1)} %reshape.445, f32[1,1,1,1,8,8,32,32]{7,6,5,4,3,2,1,0:T(8,128)} %mul.714, f32[1,1,1,1,8,8,32,32]{7,6,5,4,3,2,1,0:T(8,128)} %reshape.443, ...), kind=kLoop, calls=%fused_computation.40 | loop fusion | flops 524288 | bytes 2162688 | tf_op jit(solution)/shard_map/sub | solution.py:113
  107.6 12.7 %all_to_all.48 = f32[8,1,16384]{2,1,0:T(1,128)S(1)} all-to-all(f32[8,1,16384]{2,1,0:T(1,128)S(1)} %reshape.454), channel_id=1, replica_groups=mesh['tm'=8,'row'=32] {'tm'}, dimensions={0} | all-to-all | bytes 1048576 | tf_op jit(solution)/shard_map/all_to_all | solution.py:120
  120.8 1.9 reduce
  125.0 3.1 reshape.456
  128.2 11.0 %all-to-all-start.2 = ((f32[32,1,4096]{2,1,0:T(1,128)}), f32[32,1,4096]{2,1,0:T(1,128)S(1)}, u32[]{:S(2)}, u32[]{:S(2)}) async-start(f32[32,1,4096]{2,1,0:T(1,128)} %reshape.456), calls=%async_computation.2 | async-start | bytes 1048576 | tf_op jit(solution)/shard_map/all_to_all | solution.py:119
  139.2 16.5 %all-to-all-done.2 = f32[32,1,4096]{2,1,0:T(1,128)S(1)} async-done(((f32[32,1,4096]{2,1,0:T(1,128)}), f32[32,1,4096]{2,1,0:T(1,128)S(1)}, u32[]{:S(2)}, u32[]{:S(2)}) %all-to-all-start.2) | async-done | bytes 524320 | tf_op jit(solution)/shard_map/all_to_all | solution.py:119
  155.7 1.9 reduce.1
  158.9 74.5 %fusion.10 = f32[32,2048]{1,0:T(8,128)S(1)} fusion(f32[2048,32]{1,0:T(8,128)S(1)} %bitcast.96), kind=kOutput, calls=%fused_computation.14 | convolution fusion | flops 1669332992 | bytes 524288 | tf_op jit(solution)/shard_map/rxf,xq->rfq/dot_general | solution.py:130
  233.4 74.7 %fusion.8 = f32[32,2048]{1,0:T(8,128)S(1)} fusion(f32[2048,32]{1,0:T(8,128)S(1)} %bitcast.98), kind=kOutput, calls=%fused_computation.13 | convolution fusion | flops 1669332992 | bytes 524288 | tf_op jit(solution)/shard_map/rxf,xq->rfq/dot_general | solution.py:133
  308.1 75.3 %fusion.19 = f32[32,2048]{1,0:T(8,128)S(1)} fusion(f32[32,2048]{1,0:T(8,128)S(1)} %fusion.10, f32[2048,32]{1,0:T(8,128)S(1)} %bitcast.99), kind=kOutput, calls=%fused_computation.18 | convolution fusion | flops 1669464064 | bytes 786432 | tf_op jit(solution)/shard_map/rxf,xq->rfq/dot_general | solution.py:130
  383.4 75.3 %subtract_bitcast_fusion = (f32[1,1,32,2048]{3,2,1,0:T(8,128)S(1)}, f32[1,1,32,2048]{3,2,1,0:T(8,128)S(1)}) fusion(f32[32,2048]{1,0:T(8,128)S(1)} %fusion.19, f32[32]{0:T(128)S(1)} %get-tuple-element.136, f32[2048]{0:T(1024)S(1)} %multiply_multiply_fusion.2, f32[32]{0:T(128)S(1)} %get-tuple-element.135, f32[32,2048]{1,0:T(8,128)S(1)} %fusion.8, ...), kind=kOutput, calls=%fused_computation.58 | convolution fusion | flops 1669988352 | bytes 1319168 | tf_op jit(solution)/shard_map/rxf,xq->rfq/dot_general | solution.py:133
  (77 shorter events, 35.9 us)
Async XLA Ops:
  4.0 1.0 copy-start.3
  5.2 23.4 %copy-start.6 = (f32[1,64]{1,0:T(1,128)S(1)}, f32[1,64]{1,0:T(1,128)}, u32[]{:S(2)}) copy-start(f32[1,64]{1,0:T(1,128)} %param.5) | copy-start | bytes 772
  5.2 23.4 %copy-start.1 = (f32[1,64,2048]{2,1,0:T(8,128)S(1)}, f32[1,64,2048]{2,1,0:T(8,128)}, u32[]{:S(2)}) copy-start(f32[1,64,2048]{2,1,0:T(8,128)} %param.4) | copy-start | bytes 1572868
  32.7 26.4 %all-to-all-start = ((f32[3,1,64,2048]{3,1,0,2:T(1,128)}), f32[3,1,64,2048]{3,1,0,2:T(1,128)S(1)}, u32[]{:S(2)}, u32[]{:S(2)}) async-start(f32[3,1,64,2048]{3,1,0,2:T(1,128)} %pad_maximum_fusion.1), calls=%async_computation | async-start | bytes 3145728 | tf_op jit(solution)/shard_map/all_to_all | solution.py:104
  65.6 0.8 copy-start
  91.7 5.1 %copy-start.4 = (f32[8,64,128]{2,1,0:T(8,128)S(1)}, f32[8,64,128]{2,1,0:T(8,128)}, u32[]{:S(2)}) copy-start(f32[8,64,128]{2,1,0:T(8,128)} %fusion.49) | copy-start | bytes 786436
  95.5 2.1 copy-start.2
  95.5 2.1 copy-start.5
  128.2 27.6 %all-to-all-start.2 = ((f32[32,1,4096]{2,1,0:T(1,128)}), f32[32,1,4096]{2,1,0:T(1,128)S(1)}, u32[]{:S(2)}, u32[]{:S(2)}) async-start(f32[32,1,4096]{2,1,0:T(1,128)} %reshape.456), calls=%async_computation.2 | async-start | bytes 1048576 | tf_op jit(solution)/shard_map/all_to_all | solution.py:119
where the time goes:
time: 465 us; the launch traced here: 460 us
  matrix products  326 us (70%)
  waiting for transfers between devices  37.6 us (8%)
  blocking collectives  33.1 us (7%)
  local copies, waits for them, and re-layouts  25 us (5%)
  other arithmetic  22.7 us (5%)
  starting transfers between devices  15.1 us (3%)
    dot_general x1, matrix products, per_device(): jnp.einsum('rxf,xq->rfq', imag_part, sin_full, precision=highest)  75.3 us
    dot_general x1, matrix products, per_device(): jnp.einsum('rxf,xq->rfq', real_part, sin_full, precision=highest)  75.3 us
    dot_general x1, matrix products, per_device(): jnp.einsum('rxf,xq->rfq', imag_part, cos_full, precision=highest)  74.7 us
    dot_general x1, matrix products, per_device(): jnp.einsum('rxf,xq->rfq', real_part, cos_full, precision=highest)  74.5 us
    all_to_all x1, waiting for transfers between devices, per_device(): lax.all_to_all(stacked, 'tm', split_axis=2, concat_axis=3, tiled=True)  21.1 us
    all_gather x1, blocking collectives, carried_in(): everything = lax.all_gather(value, axis)  20.4 us
    all_to_all x1, waiting for transfers between devices, per_device(): lax.all_to_all(lax.all_to_all(packed, 'tm', split_axis=5, concat_axis=3,...  16.5 us
    all_to_all x1, blocking collectives, per_device(): lax.all_to_all(packed, 'tm', split_axis=5, concat_axis=3, tiled=True)  12.7 us
  transfers between devices with their start and end apart: 2, of which 2 were waited for; matrix products, arithmetic and copies ran while one was open for 0% of the time, Pallas kernels for 0%

commit v1 on v0

v1 whole, which is shorter than its diff:
```python
import math

import jax
import jax.numpy as jnp
import ml_dtypes
import numpy as np
from jax import lax
from jax.experimental import pallas as pl
from jax.experimental.pallas import tpu as pltpu
from jax.sharding import PartitionSpec as P

NX = 2048
NT = 16384
NF = 8192

kerr_coeff = 0.3
ionize_rate = 0.4

F32 = jnp.float32
BF16 = jnp.bfloat16


def two_parts(table):
    high = table.astype(ml_dtypes.bfloat16)
    low = (table - high.astype(np.float64)).astype(ml_dtypes.bfloat16)
    return high, low


def turns(left, right, period):
    product = (np.asarray(left)[:, None] * np.asarray(right)[None, :]) % period
    angle = product.astype(np.float64) * (2.0 * math.pi / period)
    return np.cos(angle), np.sin(angle)


def time_tables():
    index = np.arange(128)
    cos_one, sin_one = turns(index, index, 128)
    one_high, one_low = two_parts(np.concatenate([cos_one, -sin_one], 0))
    one = np.concatenate([one_high, one_high, one_low], 1)
    cos_twist, sin_twist = turns(index, index, NT)
    twist = np.stack([cos_twist, sin_twist]).astype(np.float32)
    cos_two, sin_two = turns(np.arange(64), index, 128)
    scale = 1.0 / math.sqrt(NT)
    two = np.block([[cos_two, sin_two], [-sin_two, cos_two]]) * scale
    two_high, two_low = two_parts(two)
    two = np.concatenate([two_high, two_low], 0)
    within = (index[:, None] <= index[None, :]).astype(np.float64)
    within = np.concatenate([within, np.ones((128, 128))], 1)
    within = np.concatenate([within, within], 0).astype(ml_dtypes.bfloat16)
    earlier = (index[None, :] < index[:, None]).astype(np.float64)
    earlier = np.concatenate([earlier, earlier], 1).astype(ml_dtypes.bfloat16)
    return one, twist, two, within, earlier


def cross_tables():
    order = np.arange(128)
    x_hi = (order % 32) * 4 + order // 32
    cos_one, sin_one = turns(x_hi, np.arange(128), 128)
    scale = 1.0 / math.sqrt(NX)
    table = np.block([[cos_one, -sin_one], [sin_one, cos_one]]) * scale
    high, low = two_parts(table)
    cos_twist, sin_twist = turns(np.arange(16), np.arange(128), NX)
    twist = np.stack([cos_twist, sin_twist]).astype(np.float32)
    return np.stack([high, low]), twist


def split(value):
    high = value.astype(BF16)
    low = (value - high.astype(F32)).astype(BF16)
    return high, low


def dot(left, right):
    return jnp.dot(left, right, preferred_element_type=F32)


def dot_nt(left, right):
    return lax.dot_general(left, right, (((1,), (1,)), ((), ())), preferred_element_type=F32)


def time_kernel(
    place_ref,
    screen_ref,
    x_ref,
    one_ref,
    twist_ref,
    two_ref,
    within_ref,
    earlier_ref,
    out_ref,
    high_ref,
    low_ref,
):
    first_point = place_ref[0] * 8
    cos_twist = twist_ref[0]
    sin_twist = twist_ref[1]
    for p in range(8):
        sample = x_ref[pl.ds(p, 128, stride=8), :]
        square = sample * sample
        fourth_high, fourth_low = split(square * square)
        sums = dot(jnp.concatenate([fourth_high, fourth_low], 1), within_ref[...])
        total_high, total_low = split(sums[:, 128:])
        before = dot(earlier_ref[...], jnp.concatenate([total_high, total_low], 0))
        density = (sums[:, :128] + before) * (ionize_rate / NT)
        strength = 2.0 * screen_ref[first_point + p]
        polarization = (kerr_coeff * square + strength) * sample
        current = density * sample
        signals = jnp.concatenate([sample, polarization, current], 1)
        signal_high, signal_low = split(signals)
        stack = jnp.concatenate([signal_high, signal_low, signal_high], 0)
        first = dot(one_ref[...], stack)
        for s in range(3):
            re = first[:128, s * 128 : (s + 1) * 128]
            im = first[128:, s * 128 : (s + 1) * 128]
            turned = jnp.concatenate(
                [re * cos_twist + im * sin_twist, im * cos_twist - re * sin_twist], 1
            )
            high, low = split(turned)
            for c in range(4):
                rows = pl.ds((c * 8 + p) * 32, 32)
                high_ref[s, rows, :] = high[c * 32 : (c + 1) * 32]
                low_ref[s, rows, :] = low[c * 32 : (c + 1) * 32]
    k2 = lax.broadcasted_iota(jnp.int32, (64, 128), 0)
    lane = lax.broadcasted_iota(jnp.int32, (64, 128), 1)
    for c in range(4):
        rows = pl.ds(c * 256, 256)
        parts = []
        for s in range(3):
            both = dot_nt(two_ref[...], high_ref[s, rows, :])
            rest = dot_nt(two_ref[:128], low_ref[s, rows, :])
            value = both[:128] + both[128:] + rest
            parts.append((value[:64], value[64:]))
        scaled = (k2 * 128 + c * 32 + lane % 32).astype(F32) / NF
        kerr = 0.2 * scaled
        plasma = 0.5 / (1.0 + 64.0 * scaled * scaled)
        for h in range(2):
            cut = slice(h * 128, (h + 1) * 128)
            (base_re, base_im), (kerr_re, kerr_im), (plasma_re, plasma_im) = [
                (re[:, cut], im[:, cut]) for re, im in parts
            ]
            mixed_re = base_re - kerr * kerr_im - plasma * plasma_re
            mixed_im = base_im + kerr * kerr_re - plasma * plasma_im
            out_ref[pl.ds(c * 4 + h, 64, stride=16), :] = mixed_re
            out_ref[pl.ds(c * 4 + 2 + h, 64, stride=16), :] = mixed_im


def fft4(values):
    (ar, ai), (br, bi), (cr, ci), (dr, di) = values
    sr, si, tr, ti = ar + cr, ai + ci, ar - cr, ai - ci
    ur, ui, vr, vi = br + dr, bi + di, br - dr, bi - di
    return [(sr + ur, si + ui), (tr + vi, ti - vr), (sr - ur, si - ui), (tr - vi, ti + vr)]


def fft16(values):
    columns = []
    for n in range(4):
        column = fft4([values[4 * m + n] for m in range(4)])
        turned = []
        for k, (re, im) in enumerate(column):
            step = n * k
            if step == 0:
                turned.append((re, im))
            elif step == 4:
                turned.append((im, -re))
            else:
                c = math.cos(2 * math.pi * step / 16)
                s = math.sin(2 * math.pi * step / 16)
                turned.append((re * c + im * s, im * c - re * s))
        columns.append(turned)
    result = [None] * 16
    for k in range(4):
        for m, value in enumerate(fft4([columns[n][k] for n in range(4)])):
            result[k + 4 * m] = value
    return result


def cos_sin(angle):
    quarter = jnp.round(angle * (2.0 / math.pi))
    rest = angle - quarter * 1.5703125
    rest = rest - quarter * 4.837512969970703125e-4
    rest = rest - quarter * 7.54978995489188216e-8
    square = rest * rest
    sine = rest + rest * square * (
        -1.6666654611e-1 + square * (8.3321608736e-3 + square * -1.9515295891e-4)
    )
    cosine = (
        1.0
        - 0.5 * square
        + square
        * square
        * (4.166664568298827e-2 + square * (-1.388731625493765e-3 + square * 2.443315711809948e-5))
    )
    which = quarter.astype(jnp.int32) & 3
    odd = (which & 1) == 1
    cos_out = jnp.where(odd, sine, cosine)
    sin_out = jnp.where(odd, cosine, sine)
    cos_out = jnp.where((which == 1) | (which == 2), -cos_out, cos_out)
    sin_out = jnp.where(which >= 2, -sin_out, sin_out)
    return cos_out, sin_out


def cross_kernel(place_ref, x_ref, table_ref, twist_ref, out_ref, hold_ref):
    grids = []
    for part in range(2):
        columns = []
        for odd in range(2):
            for h in range(2):
                j = part * 2 + h
                pieces = [
                    x_ref[pl.ds((2 * pair + odd) * 128 + j, 32, stride=4), :] for pair in range(4)
                ]
                columns.append(jnp.concatenate(pieces, 0).T)
        grids.append(jnp.concatenate(columns, 0))
    high, low = split(jnp.concatenate(grids, 1))
    hold_ref[...] = dot(high, table_ref[0]) + dot(low, table_ref[0]) + dot(high, table_ref[1])
    first_bin = (place_ref[0] * 32 + place_ref[1]) * 32
    bins = lax.broadcasted_iota(jnp.int32, (8, 128), 0)
    lane = lax.broadcasted_iota(jnp.int32, (8, 128), 1)
    for tile in range(4):
        values = []
        for n in range(16):
            rows = pl.ds(n * 32 + tile * 8, 8)
            re = hold_ref[rows, :128]
            im = hold_ref[rows, 128:]
            c = twist_ref[0, n : n + 1, :]
            s = twist_ref[1, n : n + 1, :]
            values.append((re * c + im * s, im * c - re * s))
        scaled = (first_bin + tile * 8 + bins).astype(F32) / NF
        forward = 40.0 * scaled * (1.0 + 0.3 * scaled * scaled)
        for m, (re, im) in enumerate(fft16(values)):
            q = lane + m * 128
            transverse = jnp.where(q < NX // 2, q, q - NX).astype(F32) / (NX // 2)
            angle = forward - 20.0 * transverse * transverse / (scaled + 0.05)
            c, s = cos_sin(angle)
            out_ref[0, pl.ds(tile * 8, 8), m * 128 : (m + 1) * 128] = re * c - im * s
            out_ref[1, pl.ds(tile * 8, 8), m * 128 : (m + 1) * 128] = re * s + im * c


def time_part(place, screen, samples):
    tables = time_tables()
    in_vmem = pl.BlockSpec(memory_space=pltpu.VMEM)
    in_smem = pl.BlockSpec(memory_space=pltpu.SMEM)
    return pl.pallas_call(
        time_kernel,
        out_shape=jax.ShapeDtypeStruct((1024, 128), F32),
        in_specs=[in_smem, in_smem] + [in_vmem] * 6,
        out_specs=in_vmem,
        scratch_shapes=[pltpu.VMEM((3, 1024, 256), BF16)] * 2,
        compiler_params=pltpu.CompilerParams(vmem_limit_bytes=32 * 2**20),
        name="time_spectra",
    )(place, screen, samples, *tables)


def cross_part(place, blocks):
    tables = cross_tables()
    in_vmem = pl.BlockSpec(memory_space=pltpu.VMEM)
    in_smem = pl.BlockSpec(memory_space=pltpu.SMEM)
    return pl.pallas_call(
        cross_kernel,
        out_shape=jax.ShapeDtypeStruct((2, 32, NX), F32),
        in_specs=[in_smem] + [in_vmem] * 3,
        out_specs=in_vmem,
        scratch_shapes=[pltpu.VMEM((512, 256), F32)],
        compiler_params=pltpu.CompilerParams(vmem_limit_bytes=32 * 2**20),
        name="cross_spectra",
    )(place, blocks, *tables)


def per_device(field, screen):
    place = jnp.stack([lax.axis_index("tm"), lax.axis_index("row")]).astype(jnp.int32)
    mine = field.reshape(8, 8, 16, 128).transpose(0, 2, 1, 3)
    samples = lax.all_to_all(mine, "tm", split_axis=0, concat_axis=0, tiled=True)
    mixed = time_part(place, screen.reshape(64), samples.reshape(1024, 128))
    blocks = lax.all_to_all(
        mixed.reshape(256, 4, 128), ("tm", "row"), split_axis=0, concat_axis=0, tiled=True
    )
    return cross_part(place, blocks.reshape(1024, 128)).reshape(2, 1, 32, NX)


def solution(mesh):
    return jax.shard_map(
        per_device,
        mesh=mesh,
        in_specs=(P(None, "row", "tm"), P(None, "row")),
        out_specs=P(None, None, ("tm", "row"), None),
        check_vma=False,
    )
```

time: 465 us -> 58.2 us (0.13); the launches traced: 460 us -> 58 us
  matrix products: 326 us -> 0 us
  waiting for transfers between devices: 37.6 us -> 11.6 us
  local copies, waits for them, and re-layouts: 25 us -> 0.66 us
  other arithmetic: 22.7 us -> 0.07 us
  starting transfers between devices: 15.1 us -> 7.62 us
  Pallas kernels: 0 us -> 7.23 us
    dot_general x23 -> x0, matrix products: 326 us -> none  [the longest x1 75.3 us: per_device(): jnp.einsum('rxf,xq->rfq', imag_part, sin_full, precision=highest)]
    all_to_all x2 -> x1, waiting for transfers between devices: 37.6 us -> 11.6 us  [per_device(): lax.all_to_all(mine, 'tm', split_axis=0, concat_axis=0, tiled=True)]
    all_gather x1 -> x0, blocking collectives: 20.4 us -> none  [carried_in(): everything = lax.all_gather(value, axis)]
    all_to_all x1, blocking collectives: 12.7 us -> 30.7 us  [per_device(): lax.all_to_all(mixed.reshape(256, 4, 128), ('tm', 'row'), split_axis=0, c...]
    sub x1 -> x0, other arithmetic: 8.78 us -> none  [per_device(): mixed_re = base_re - weight_kerr * kerr_im - weight_plasma * plasma_re]
    unnamed x19 -> x16, local copies, waits for them, and re-layouts: 8.79 us -> 0.66 us
    all_to_all x2 -> x1, starting transfers between devices: 15.1 us -> 7.62 us  [per_device(): lax.all_to_all(mine, 'tm', split_axis=0, concat_axis=0, tiled=True)]
    reshape x5 -> x0, local copies, waits for them, and re-layouts: 7.31 us -> none  [the longest x4 6.96 us: time_spectrum(): return (spec_re.reshape(target) * factor, spec_im.reshape(target) * factor)]
  transfers between devices with their start and end apart: 2 -> 1, of which waited for: 2 -> 1; matrix products, arithmetic and copies ran while one was open for 0% -> 0% of each run, Pallas kernels for 0% -> 0%
where the time goes in v1:
time: 58.2 us; the launch traced here: 58 us
  blocking collectives  30.7 us (53%)
  waiting for transfers between devices  11.6 us (20%)
  starting transfers between devices  7.62 us (13%)
  Pallas kernels  7.23 us (12%)
  local copies, waits for them, and re-layouts  0.66 us (1%)
    all_to_all x1, blocking collectives, per_device(): lax.all_to_all(mixed.reshape(256, 4, 128), ('tm', 'row'), split_axis=0, c...  30.7 us
    all_to_all x1, waiting for transfers between devices, per_device(): lax.all_to_all(mine, 'tm', split_axis=0, concat_axis=0, tiled=True)  11.6 us
    all_to_all x1, starting transfers between devices, per_device(): lax.all_to_all(mine, 'tm', split_axis=0, concat_axis=0, tiled=True)  7.62 us
    pallas_call x1, Pallas kernels, time_part(): pl.pallas_call(time_kernel, out_shape=jax.ShapeDtypeStruct((1024, 128), F...  4.97 us
    pallas_call x1, Pallas kernels, cross_part(): pl.pallas_call(cross_kernel, out_shape=jax.ShapeDtypeStruct((2, 32, NX),...  2.26 us
  transfers between devices with their start and end apart: 1, of which 1 were waited for; matrix products, arithmetic and copies ran while one was open for 0% of the time, Pallas kernels for 0%

profile of v1, /device:TPU:1, one launch (start us, length us, event | category | flops | bytes accessed | tf_op | source)
XLA Modules:
  0.0 58.0 jit_solution(1232763798190171747)
XLA Ops:
  0.0 0.0 copy-start.1
  0.0 0.0 copy-start.2
  0.0 0.0 copy-start.3
  0.0 0.0 copy-start.4
  0.0 0.0 copy-start.5
  0.0 7.6 %all-to-all-start = ((f32[8,16,8,128]{3,2,1,0:T(8,128)}), f32[8,16,8,128]{3,2,1,0:T(8,128)S(1)}, u32[]{:S(2)}, u32[]{:S(2)}) async-start(f32[8,16,8,128]{3,2,1,0:T(8,128)} %bitcast.16), calls=%async_computation | async-start | bytes 1048576 | tf_op jit(solution)/shard_map/all_to_all | solution.py:272
  7.7 0.1 pad_add_fusion.place_ref
  7.7 11.6 %all-to-all-done = f32[8,16,8,128]{3,2,1,0:T(8,128)S(1)} async-done(((f32[8,16,8,128]{3,2,1,0:T(8,128)}), f32[8,16,8,128]{3,2,1,0:T(8,128)S(1)}, u32[]{:S(2)}, u32[]{:S(2)}) %all-to-all-start) | async-done | bytes 524320 | tf_op jit(solution)/shard_map/all_to_all | solution.py:272
  19.4 0.0 copy-start.7
  19.4 0.0 copy-done.1
  19.4 0.0 copy-done.2
  19.4 0.0 copy-done.3
  19.4 0.0 copy-done.4
  19.4 0.0 copy-done.5
  19.4 0.6 %copy-done.7 = f32[1,64]{1,0:T(1,128)S(1)} copy-done((f32[1,64]{1,0:T(1,128)S(1)}, f32[1,64]{1,0:T(1,128)}, u32[]{:S(2)}) %copy-start.7) | copy-done | bytes 280
  20.0 5.0 %time_spectra.1 = f32[1024,128]{1,0:T(8,128)S(1)} custom-call(s32[2]{0:T(128)S(1)} %pad_add_fusion.place_ref, f32[64]{0:T(128)S(1)} %bitcast.15, f32[1024,128]{1,0:T(8,128)S(1)} %bitcast.12, bf16[256,384]{1,0:T(8,128)(2,1)S(1)} %copy-done.1, f32[2,128,128]{2,1,0:T(8,128)S(1)} %copy-done.4, bf16[256,256]{1,0:T(8,128)(2,1)S(1)} %copy-done.3, ...), custom_call_target="tpu_custom_call" | custom-call | tf_op jit(solution)/shard_map/time_spectra/pallas_call | solution.py:243
  25.0 0.0 copy-start
  25.0 0.0 copy-start.6
  25.0 30.7 %all_to_all.10 = f32[256,4,128]{2,1,0:T(4,128)S(1)} all-to-all(f32[256,4,128]{2,1,0:T(4,128)S(1)} %bitcast.13), channel_id=1, replica_groups=mesh['tm'=8,'row'=32] {'tm','row'}, dimensions={0} | all-to-all | bytes 1048576 | tf_op jit(solution)/shard_map/all_to_all | solution.py:274
  55.7 0.0 copy-done
  55.7 0.0 copy-done.6
  55.7 2.3 %cross_spectra.1 = f32[2,32,2048]{2,1,0:T(8,128)} custom-call(s32[2]{0:T(128)S(1)} %pad_add_fusion.place_ref, f32[1024,128]{1,0:T(8,128)S(1)} %bitcast.14, bf16[2,256,256]{2,1,0:T(8,128)(2,1)S(1)} %copy-done, f32[2,16,128]{2,1,0:T(8,128)S(1)} %copy-done.6), custom_call_target="tpu_custom_call" | custom-call | tf_op jit(solution)/shard_map/cross_spectra/pallas_call | solution.py:258
Async XLA Ops:
  0.0 19.4 %copy-start.1 = (bf16[256,384]{1,0:T(8,128)(2,1)S(1)}, bf16[256,384]{1,0:T(8,128)(2,1)}, u32[]{:S(2)}) copy-start(bf16[256,384]{1,0:T(8,128)(2,1)} %constant.23.clone.one_ref) | copy-start | bytes 589828
  0.0 19.4 %copy-start.2 = (bf16[256,256]{1,0:T(8,128)(2,1)S(1)}, bf16[256,256]{1,0:T(8,128)(2,1)}, u32[]{:S(2)}) copy-start(bf16[256,256]{1,0:T(8,128)(2,1)} %constant.26.clone.within_ref) | copy-start | bytes 393220
  0.0 19.4 %copy-start.3 = (bf16[256,256]{1,0:T(8,128)(2,1)S(1)}, bf16[256,256]{1,0:T(8,128)(2,1)}, u32[]{:S(2)}) copy-start(bf16[256,256]{1,0:T(8,128)(2,1)} %constant.25.clone.two_ref) | copy-start | bytes 393220
  0.0 19.4 %copy-start.4 = (f32[2,128,128]{2,1,0:T(8,128)S(1)}, f32[2,128,128]{2,1,0:T(8,128)}, u32[]{:S(2)}) copy-start(f32[2,128,128]{2,1,0:T(8,128)} %constant.24.clone.twist_ref) | copy-start | bytes 393220
  0.0 19.4 %copy-start.5 = (bf16[128,256]{1,0:T(8,128)(2,1)S(1)}, bf16[128,256]{1,0:T(8,128)(2,1)}, u32[]{:S(2)}) copy-start(bf16[128,256]{1,0:T(8,128)(2,1)} %constant.27.clone.earlier_ref) | copy-start | bytes 196612
  0.0 19.3 %all-to-all-start = ((f32[8,16,8,128]{3,2,1,0:T(8,128)}), f32[8,16,8,128]{3,2,1,0:T(8,128)S(1)}, u32[]{:S(2)}, u32[]{:S(2)}) async-start(f32[8,16,8,128]{3,2,1,0:T(8,128)} %bitcast.16), calls=%async_computation | async-start | bytes 1048576 | tf_op jit(solution)/shard_map/all_to_all | solution.py:272
  19.4 0.7 %copy-start.7 = (f32[1,64]{1,0:T(1,128)S(1)}, f32[1,64]{1,0:T(1,128)}, u32[]{:S(2)}) copy-start(f32[1,64]{1,0:T(1,128)} %param.10) | copy-start | bytes 772
  25.0 30.7 %copy-start = (bf16[2,256,256]{2,1,0:T(8,128)(2,1)S(1)}, bf16[2,256,256]{2,1,0:T(8,128)(2,1)}, u32[]{:S(2)}) copy-start(bf16[2,256,256]{2,1,0:T(8,128)(2,1)} %constant.28.clone.table_ref) | copy-start | bytes 786436
  25.0 30.7 %copy-start.6 = (f32[2,16,128]{2,1,0:T(8,128)S(1)}, f32[2,16,128]{2,1,0:T(8,128)}, u32[]{:S(2)}) copy-start(f32[2,16,128]{2,1,0:T(8,128)} %constant.29.clone.twist_ref) | copy-start | bytes 49156

commit v2 on v1

--- a/solution.py
+++ b/solution.py
@@ -78,9 +78,11 @@
     return lax.dot_general(left, right, (((1,), (1,)), ((), ())), preferred_element_type=F32)
 
 
+PAIRS = 2
+
+
 def time_kernel(
-    place_ref,
-    screen_ref,
+    strength_ref,
     x_ref,
     one_ref,
     twist_ref,
@@ -90,28 +92,41 @@
     out_ref,
     high_ref,
     low_ref,
+    stack_ref,
 ):
-    first_point = place_ref[0] * 8
-    cos_twist = twist_ref[0]
-    sin_twist = twist_ref[1]
-    for p in range(8):
+    points = range(8)
+    fourths = []
+    for p in points:
         sample = x_ref[pl.ds(p, 128, stride=8), :]
         square = sample * sample
-        fourth_high, fourth_low = split(square * square)
-        sums = dot(jnp.concatenate([fourth_high, fourth_low], 1), within_ref[...])
-        total_high, total_low = split(sums[:, 128:])
-        before = dot(earlier_ref[...], jnp.concatenate([total_high, total_low], 0))
-        density = (sums[:, :128] + before) * (ionize_rate / NT)
-        strength = 2.0 * screen_ref[first_point + p]
-        polarization = (kerr_coeff * square + strength) * sample
+        fourths.append(jnp.concatenate(split(square * square), 1))
+    sums = dot(jnp.concatenate(fourths, 0), within_ref[...])
+    totals = [jnp.concatenate(split(sums[p * 128 : (p + 1) * 128, 128:]), 0) for p in points]
+    before = dot(earlier_ref[...], jnp.concatenate(totals, 1))
+    for p in points:
+        cut = slice(p * 128, (p + 1) * 128)
+        sample = x_ref[pl.ds(p, 128, stride=8), :]
+        square = sample * sample
+        density = (sums[cut, :128] + before[:, cut]) * (ionize_rate / NT)
+        polarization = (kerr_coeff * square + strength_ref[p : p + 1, :]) * sample
         current = density * sample
-        signals = jnp.concatenate([sample, polarization, current], 1)
-        signal_high, signal_low = split(signals)
-        stack = jnp.concatenate([signal_high, signal_low, signal_high], 0)
-        first = dot(one_ref[...], stack)
-        for s in range(3):
-            re = first[:128, s * 128 : (s + 1) * 128]
-            im = first[128:, s * 128 : (s + 1) * 128]
+        for s, signal in enumerate((sample, polarization, current)):
+            high, low = split(signal)
+            lanes = slice((p * 3 + s) * 128, (p * 3 + s + 1) * 128)
+            stack_ref[:128, lanes] = high
+            stack_ref[128:, lanes] = low
+    for pair in range(PAIRS):
+        width = 3072 // PAIRS
+        lanes = slice(pair * width, (pair + 1) * width)
+        first = dot(one_ref[:, :256], stack_ref[:, lanes]) + dot(
+            one_ref[:, 256:], stack_ref[:128, lanes]
+        )
+        for n in range(width // 128):
+            p, s = divmod(pair * (width // 128) + n, 3)
+            re = first[:128, n * 128 : (n + 1) * 128]
+            im = first[128:, n * 128 : (n + 1) * 128]
+            cos_twist = twist_ref[0]
+            sin_twist = twist_ref[1]
             turned = jnp.concatenate(
                 [re * cos_twist + im * sin_twist, im * cos_twist - re * sin_twist], 1
             )
@@ -199,7 +214,7 @@
     return cos_out, sin_out
 
 
-def cross_kernel(place_ref, x_ref, table_ref, twist_ref, out_ref, hold_ref):
+def cross_kernel(x_ref, table_ref, twist_ref, out_ref, hold_ref, done_ref, sem):
     grids = []
     for part in range(2):
         columns = []
@@ -209,13 +224,15 @@
                 pieces = [
                     x_ref[pl.ds((2 * pair + odd) * 128 + j, 32, stride=4), :] for pair in range(4)
                 ]
-                columns.append(jnp.concatenate(pieces, 0).T)
-        grids.append(jnp.concatenate(columns, 0))
-    high, low = split(jnp.concatenate(grids, 1))
+                columns.append(jnp.concatenate(pieces, 0))
+        grids.append(jnp.concatenate(columns, 1))
+    high, low = split(jnp.concatenate(grids, 0))
+    high, low = high.T, low.T
     hold_ref[...] = dot(high, table_ref[0]) + dot(low, table_ref[0]) + dot(high, table_ref[1])
-    first_bin = (place_ref[0] * 32 + place_ref[1]) * 32
+    first_bin = lax.axis_index(("tm", "row")) * 32
     bins = lax.broadcasted_iota(jnp.int32, (8, 128), 0)
     lane = lax.broadcasted_iota(jnp.int32, (8, 128), 1)
+    copies = []
     for tile in range(4):
         values = []
         for n in range(16):
@@ -232,49 +249,57 @@
             transverse = jnp.where(q < NX // 2, q, q - NX).astype(F32) / (NX // 2)
             angle = forward - 20.0 * transverse * transverse / (scaled + 0.05)
             c, s = cos_sin(angle)
-            out_ref[0, pl.ds(tile * 8, 8), m * 128 : (m + 1) * 128] = re * c - im * s
-            out_ref[1, pl.ds(tile * 8, 8), m * 128 : (m + 1) * 128] = re * s + im * c
-
-
-def time_part(place, screen, samples):
+            done_ref[0, pl.ds(tile * 8, 8), m * 128 : (m + 1) * 128] = re * c - im * s
+            done_ref[1, pl.ds(tile * 8, 8), m * 128 : (m + 1) * 128] = re * s + im * c
+        rows = pl.ds(tile * 8, 8)
+        copy = pltpu.make_async_copy(done_ref.at[:, rows], out_ref.at[:, rows], sem.at[tile])
+        copy.start()
+        copies.append(copy)
+    for copy in copies:
+        copy.wait()
+
+
+def time_part(strength, samples):
     tables = time_tables()
     in_vmem = pl.BlockSpec(memory_space=pltpu.VMEM)
-    in_smem = pl.BlockSpec(memory_space=pltpu.SMEM)
     return pl.pallas_call(
         time_kernel,
         out_shape=jax.ShapeDtypeStruct((1024, 128), F32),
-        in_specs=[in_smem, in_smem] + [in_vmem] * 6,
+        in_specs=[in_vmem] * 7,
         out_specs=in_vmem,
-        scratch_shapes=[pltpu.VMEM((3, 1024, 256), BF16)] * 2,
+        scratch_shapes=[pltpu.VMEM((3, 1024, 256), BF16)] * 2 + [pltpu.VMEM((256, 3072), BF16)],
         compiler_params=pltpu.CompilerParams(vmem_limit_bytes=32 * 2**20),
         name="time_spectra",
-    )(place, screen, samples, *tables)
-
-
-def cross_part(place, blocks):
+    )(strength, samples, *tables)
+
+
+def cross_part(blocks):
     tables = cross_tables()
     in_vmem = pl.BlockSpec(memory_space=pltpu.VMEM)
-    in_smem = pl.BlockSpec(memory_space=pltpu.SMEM)
     return pl.pallas_call(
         cross_kernel,
         out_shape=jax.ShapeDtypeStruct((2, 32, NX), F32),
-        in_specs=[in_smem] + [in_vmem] * 3,
-        out_specs=in_vmem,
-        scratch_shapes=[pltpu.VMEM((512, 256), F32)],
+        in_specs=[in_vmem] * 3,
+        out_specs=pl.BlockSpec(memory_space=pl.ANY),
+        scratch_shapes=[
+            pltpu.VMEM((512, 256), F32),
+            pltpu.VMEM((2, 32, NX), F32),
+            pltpu.SemaphoreType.DMA((4,)),
+        ],
         compiler_params=pltpu.CompilerParams(vmem_limit_bytes=32 * 2**20),
         name="cross_spectra",
-    )(place, blocks, *tables)
+    )(blocks, *tables)
 
 
 def per_device(field, screen):
-    place = jnp.stack([lax.axis_index("tm"), lax.axis_index("row")]).astype(jnp.int32)
     mine = field.reshape(8, 8, 16, 128).transpose(0, 2, 1, 3)
     samples = lax.all_to_all(mine, "tm", split_axis=0, concat_axis=0, tiled=True)
-    mixed = time_part(place, screen.reshape(64), samples.reshape(1024, 128))
+    strength = 2.0 * lax.dynamic_slice_in_dim(screen.reshape(64, 1), lax.axis_index("tm") * 8, 8)
+    mixed = time_part(jnp.broadcast_to(strength, (8, 128)), samples.reshape(1024, 128))
     blocks = lax.all_to_all(
         mixed.reshape(256, 4, 128), ("tm", "row"), split_axis=0, concat_axis=0, tiled=True
     )
-    return cross_part(place, blocks.reshape(1024, 128)).reshape(2, 1, 32, NX)
+    return cross_part(blocks.reshape(1024, 128)).reshape(2, 1, 32, NX)
 
 
 def solution(mesh):

time: 58.2 us -> 54.6 us (0.938)
  Pallas kernels: 7.23 us -> 4.23 us
  waiting for transfers between devices: 11.6 us -> 11 us
    pallas_call x1, Pallas kernels: 4.97 us -> 2.59 us  [time_part(): pl.pallas_call(time_kernel, out_shape=jax.ShapeDtypeStruct((1024, 128), F...]
    all_to_all x1, waiting for transfers between devices: 11.6 us -> 11 us  [per_device(): lax.all_to_all(mine, 'tm', split_axis=0, concat_axis=0, tiled=True)]
    pallas_call x1, Pallas kernels: 2.26 us -> 1.63 us  [cross_part(): pl.pallas_call(cross_kernel, out_shape=jax.ShapeDtypeStruct((2, 32, NX),...]
where the time goes in v2:
time: 54.6 us; the launch traced here: 54.4 us
  blocking collectives  30.7 us (56%)
  waiting for transfers between devices  11 us (20%)
  starting transfers between devices  7.62 us (14%)
  Pallas kernels  4.23 us (8%)
  local copies, waits for them, and re-layouts  0.76 us (1%)
    all_to_all x1, blocking collectives, per_device(): lax.all_to_all(mixed.reshape(256, 4, 128), ('tm', 'row'), split_axis=0, c...  30.7 us
    all_to_all x1, waiting for transfers between devices, per_device(): lax.all_to_all(mine, 'tm', split_axis=0, concat_axis=0, tiled=True)  11 us
    all_to_all x1, starting transfers between devices, per_device(): lax.all_to_all(mine, 'tm', split_axis=0, concat_axis=0, tiled=True)  7.62 us
    pallas_call x1, Pallas kernels, time_part(): pl.pallas_call(time_kernel, out_shape=jax.ShapeDtypeStruct((1024, 128), F...  2.59 us
    pallas_call x1, Pallas kernels, cross_part(): pl.pallas_call(cross_kernel, out_shape=jax.ShapeDtypeStruct((2, 32, NX),...  1.63 us
  transfers between devices with their start and end apart: 1, of which 1 were waited for; matrix products, arithmetic and copies ran while one was open for 0% of the time, Pallas kernels for 0%

profile of v2, /device:TPU:1, one launch (start us, length us, event | category | flops | bytes accessed | tf_op | source)
XLA Modules:
  0.0 54.4 jit_solution(387148873615379813)
XLA Ops:
  0.0 0.0 copy-start.1
  0.0 0.0 copy-start.2
  0.0 0.0 copy-start.3
  0.0 0.0 copy-start.4
  0.0 0.0 copy-start.5
  0.0 7.6 %all-to-all-start = ((f32[8,16,8,128]{3,2,1,0:T(8,128)}), f32[8,16,8,128]{3,2,1,0:T(8,128)S(1)}, u32[]{:S(2)}, u32[]{:S(2)}) async-start(f32[8,16,8,128]{3,2,1,0:T(8,128)} %bitcast.14), calls=%async_computation | async-start | bytes 1048576 | tf_op jit(solution)/shard_map/all_to_all | solution.py:296
  7.7 0.0 copy-start.7
  7.7 0.7 %copy-done.7 = f32[1,64]{1,0:T(1,128)S(1)} copy-done((f32[1,64]{1,0:T(1,128)S(1)}, f32[1,64]{1,0:T(1,128)}, u32[]{:S(2)}) %copy-start.7) | copy-done | bytes 280
  8.3 0.1 multiply_bitcast_fusion
  8.4 11.0 %all-to-all-done = f32[8,16,8,128]{3,2,1,0:T(8,128)S(1)} async-done(((f32[8,16,8,128]{3,2,1,0:T(8,128)}), f32[8,16,8,128]{3,2,1,0:T(8,128)S(1)}, u32[]{:S(2)}, u32[]{:S(2)}) %all-to-all-start) | async-done | bytes 524320 | tf_op jit(solution)/shard_map/all_to_all | solution.py:296
  19.4 0.1 broadcast_in_dim.2.strength_ref
  19.4 0.0 copy-done.1
  19.4 0.0 copy-done.2
  19.4 0.0 copy-done.3
  19.4 0.0 copy-done.4
  19.4 0.0 copy-done.5
  19.4 2.6 %time_spectra.1 = f32[1024,128]{1,0:T(8,128)S(1)} custom-call(f32[8,128]{1,0:T(8,128)S(1)} %broadcast_in_dim.2.strength_ref, f32[1024,128]{1,0:T(8,128)S(1)} %bitcast.11, bf16[256,384]{1,0:T(8,128)(2,1)S(1)} %copy-done.1, f32[2,128,128]{2,1,0:T(8,128)S(1)} %copy-done.4, bf16[256,256]{1,0:T(8,128)(2,1)S(1)} %copy-done.3, bf16[256,256]{1,0:T(8,128)(2,1)S(1)} %copy-done.2, ...), custom_call_target="tpu_custom_call" | custom-call | tf_op jit(solution)/shard_map/time_spectra/pallas_call | solution.py:265
  22.0 0.0 copy-start
  22.1 0.0 copy-start.6
  22.1 30.7 %all_to_all.10 = f32[256,4,128]{2,1,0:T(4,128)S(1)} all-to-all(f32[256,4,128]{2,1,0:T(4,128)S(1)} %bitcast.12), channel_id=1, replica_groups=mesh['tm'=8,'row'=32] {'tm','row'}, dimensions={0} | all-to-all | bytes 1048576 | tf_op jit(solution)/shard_map/all_to_all | solution.py:299
  52.8 0.0 copy-done
  52.8 0.0 copy-done.6
  52.8 1.6 %cross_spectra.1 = f32[2,32,2048]{2,1,0:T(8,128)} custom-call(f32[1024,128]{1,0:T(8,128)S(1)} %bitcast.13, bf16[2,256,256]{2,1,0:T(8,128)(2,1)S(1)} %copy-done, f32[2,16,128]{2,1,0:T(8,128)S(1)} %copy-done.6), custom_call_target="tpu_custom_call" | custom-call | tf_op jit(solution)/shard_map/cross_spectra/pallas_call | solution.py:279
Async XLA Ops:
  0.0 19.4 %copy-start.1 = (bf16[256,384]{1,0:T(8,128)(2,1)S(1)}, bf16[256,384]{1,0:T(8,128)(2,1)}, u32[]{:S(2)}) copy-start(bf16[256,384]{1,0:T(8,128)(2,1)} %constant.29.clone.one_ref) | copy-start | bytes 589828
  0.0 19.4 %copy-start.2 = (bf16[256,256]{1,0:T(8,128)(2,1)S(1)}, bf16[256,256]{1,0:T(8,128)(2,1)}, u32[]{:S(2)}) copy-start(bf16[256,256]{1,0:T(8,128)(2,1)} %constant.32.clone.within_ref) | copy-start | bytes 393220
  0.0 19.4 %copy-start.3 = (bf16[256,256]{1,0:T(8,128)(2,1)S(1)}, bf16[256,256]{1,0:T(8,128)(2,1)}, u32[]{:S(2)}) copy-start(bf16[256,256]{1,0:T(8,128)(2,1)} %constant.31.clone.two_ref) | copy-start | bytes 393220
  0.0 19.4 %copy-start.4 = (f32[2,128,128]{2,1,0:T(8,128)S(1)}, f32[2,128,128]{2,1,0:T(8,128)}, u32[]{:S(2)}) copy-start(f32[2,128,128]{2,1,0:T(8,128)} %constant.30.clone.twist_ref) | copy-start | bytes 393220
  0.0 19.4 %copy-start.5 = (bf16[128,256]{1,0:T(8,128)(2,1)S(1)}, bf16[128,256]{1,0:T(8,128)(2,1)}, u32[]{:S(2)}) copy-start(bf16[128,256]{1,0:T(8,128)(2,1)} %constant.33.clone.earlier_ref) | copy-start | bytes 196612
  0.0 19.3 %all-to-all-start = ((f32[8,16,8,128]{3,2,1,0:T(8,128)}), f32[8,16,8,128]{3,2,1,0:T(8,128)S(1)}, u32[]{:S(2)}, u32[]{:S(2)}) async-start(f32[8,16,8,128]{3,2,1,0:T(8,128)} %bitcast.14), calls=%async_computation | async-start | bytes 1048576 | tf_op jit(solution)/shard_map/all_to_all | solution.py:296
  7.7 0.7 %copy-start.7 = (f32[1,64]{1,0:T(1,128)S(1)}, f32[1,64]{1,0:T(1,128)}, u32[]{:S(2)}) copy-start(f32[1,64]{1,0:T(1,128)} %param.10) | copy-start | bytes 772
  22.0 30.7 %copy-start = (bf16[2,256,256]{2,1,0:T(8,128)(2,1)S(1)}, bf16[2,256,256]{2,1,0:T(8,128)(2,1)}, u32[]{:S(2)}) copy-start(bf16[2,256,256]{2,1,0:T(8,128)(2,1)} %constant.34.clone.table_ref) | copy-start | bytes 786436
  22.1 30.7 %copy-start.6 = (f32[2,16,128]{2,1,0:T(8,128)S(1)}, f32[2,16,128]{2,1,0:T(8,128)}, u32[]{:S(2)}) copy-start(f32[2,16,128]{2,1,0:T(8,128)} %constant.35.clone.twist_ref) | copy-start | bytes 49156

commit v3 on v2

--- a/solution.py
+++ b/solution.py
@@ -214,49 +214,83 @@
     return cos_out, sin_out
 
 
-def cross_kernel(x_ref, table_ref, twist_ref, out_ref, hold_ref, done_ref, sem):
-    grids = []
+def prepare_kernel(screen_ref, strength_ref, phase_ref):
+    screen = jnp.broadcast_to(jnp.concatenate([screen_ref[...]] * 2, 1), (8, 128))
+    first_point = lax.axis_index("tm") * 8
+    mine = 2.0 * pltpu.roll(screen, (128 - first_point) % 128, 1)
+    for p in range(8):
+        strength_ref[p : p + 1, :] = jnp.broadcast_to(mine[:1, p : p + 1], (1, 128))
+    first_bin = lax.axis_index(("tm", "row")) * 32
+    bins = lax.broadcasted_iota(jnp.int32, (8, 128), 0)
+    lane = lax.broadcasted_iota(jnp.int32, (8, 128), 1)
+    for tile in range(4):
+        scaled = (first_bin + tile * 8 + bins).astype(F32) / NF
+        forward = 40.0 * scaled * (1.0 + 0.3 * scaled * scaled)
+        for m in range(16):
+            q = lane + m * 128
+            transverse = jnp.where(q < NX // 2, q, q - NX).astype(F32) / (NX // 2)
+            angle = forward - 20.0 * transverse * transverse / (scaled + 0.05)
+            for part, value in enumerate(cos_sin(angle)):
+                phase_ref[part, pl.ds(tile * 8, 8), m * 128 : (m + 1) * 128] = value
+
+
+def cross_kernel(x_ref, phase_ref, table_ref, twist_ref, out_ref, done_ref, sem):
+    blocks = []
     for part in range(2):
-        columns = []
         for odd in range(2):
             for h in range(2):
                 j = part * 2 + h
                 pieces = [
                     x_ref[pl.ds((2 * pair + odd) * 128 + j, 32, stride=4), :] for pair in range(4)
                 ]
-                columns.append(jnp.concatenate(pieces, 0))
-        grids.append(jnp.concatenate(columns, 1))
-    high, low = split(jnp.concatenate(grids, 0))
-    high, low = high.T, low.T
-    hold_ref[...] = dot(high, table_ref[0]) + dot(low, table_ref[0]) + dot(high, table_ref[1])
-    first_bin = lax.axis_index(("tm", "row")) * 32
-    bins = lax.broadcasted_iota(jnp.int32, (8, 128), 0)
-    lane = lax.broadcasted_iota(jnp.int32, (8, 128), 1)
+                blocks.append(jnp.concatenate(pieces, 0).T)
     copies = []
     for tile in range(4):
+        rows = [slice(n * 32 + tile * 8, n * 32 + tile * 8 + 8) for n in range(4)]
+        grid = jnp.concatenate(
+            [
+                jnp.concatenate([blocks[part * 4 + n // 4][rows[n % 4]] for n in range(16)], 0)
+                for part in range(2)
+            ],
+            1,
+        )
+        high, low = split(grid)
+        first = dot(high, table_ref[0]) + dot(low, table_ref[0]) + dot(high, table_ref[1])
         values = []
         for n in range(16):
-            rows = pl.ds(n * 32 + tile * 8, 8)
-            re = hold_ref[rows, :128]
-            im = hold_ref[rows, 128:]
+            re = first[n * 8 : n * 8 + 8, :128]
+            im = first[n * 8 : n * 8 + 8, 128:]
             c = twist_ref[0, n : n + 1, :]
             s = twist_ref[1, n : n + 1, :]
             values.append((re * c + im * s, im * c - re * s))
-        scaled = (first_bin + tile * 8 + bins).astype(F32) / NF
-        forward = 40.0 * scaled * (1.0 + 0.3 * scaled * scaled)
+        rows = pl.ds(tile * 8, 8)
         for m, (re, im) in enumerate(fft16(values)):
-            q = lane + m * 128
-            transverse = jnp.where(q < NX // 2, q, q - NX).astype(F32) / (NX // 2)
-            angle = forward - 20.0 * transverse * transverse / (scaled + 0.05)
-            c, s = cos_sin(angle)
-            done_ref[0, pl.ds(tile * 8, 8), m * 128 : (m + 1) * 128] = re * c - im * s
-            done_ref[1, pl.ds(tile * 8, 8), m * 128 : (m + 1) * 128] = re * s + im * c
-        rows = pl.ds(tile * 8, 8)
+            lanes = slice(m * 128, (m + 1) * 128)
+            c = phase_ref[0, rows, lanes]
+            s = phase_ref[1, rows, lanes]
+            done_ref[0, rows, lanes] = re * c - im * s
+            done_ref[1, rows, lanes] = re * s + im * c
         copy = pltpu.make_async_copy(done_ref.at[:, rows], out_ref.at[:, rows], sem.at[tile])
         copy.start()
         copies.append(copy)
     for copy in copies:
         copy.wait()
+
+
+def prepare_part(screen):
+    in_vmem = pl.BlockSpec(memory_space=pltpu.VMEM)
+    return pl.pallas_call(
+        prepare_kernel,
+        out_shape=[
+            jax.ShapeDtypeStruct((8, 128), F32),
+            jax.ShapeDtypeStruct((2, 32, NX), F32),
+        ],
+        in_specs=[in_vmem],
+        out_specs=[in_vmem, in_vmem],
+        cost_estimate=pl.CostEstimate(flops=4000000, bytes_accessed=524288, transcendentals=0),
+        compiler_params=pltpu.CompilerParams(vmem_limit_bytes=16 * 2**20),
+        name="prepare",
+    )(screen)
 
 
 def time_part(strength, samples):
@@ -273,33 +307,32 @@
     )(strength, samples, *tables)
 
 
-def cross_part(blocks):
+def cross_part(blocks, phases):
     tables = cross_tables()
     in_vmem = pl.BlockSpec(memory_space=pltpu.VMEM)
     return pl.pallas_call(
         cross_kernel,
         out_shape=jax.ShapeDtypeStruct((2, 32, NX), F32),
-        in_specs=[in_vmem] * 3,
+        in_specs=[in_vmem] * 4,
         out_specs=pl.BlockSpec(memory_space=pl.ANY),
         scratch_shapes=[
-            pltpu.VMEM((512, 256), F32),
             pltpu.VMEM((2, 32, NX), F32),
             pltpu.SemaphoreType.DMA((4,)),
         ],
         compiler_params=pltpu.CompilerParams(vmem_limit_bytes=32 * 2**20),
         name="cross_spectra",
-    )(blocks, *tables)
+    )(blocks, phases, *tables)
 
 
 def per_device(field, screen):
     mine = field.reshape(8, 8, 16, 128).transpose(0, 2, 1, 3)
     samples = lax.all_to_all(mine, "tm", split_axis=0, concat_axis=0, tiled=True)
-    strength = 2.0 * lax.dynamic_slice_in_dim(screen.reshape(64, 1), lax.axis_index("tm") * 8, 8)
-    mixed = time_part(jnp.broadcast_to(strength, (8, 128)), samples.reshape(1024, 128))
+    strength, phases = prepare_part(screen)
+    mixed = time_part(strength, samples.reshape(1024, 128))
     blocks = lax.all_to_all(
         mixed.reshape(256, 4, 128), ("tm", "row"), split_axis=0, concat_axis=0, tiled=True
     )
-    return cross_part(blocks.reshape(1024, 128)).reshape(2, 1, 32, NX)
+    return cross_part(blocks.reshape(1024, 128), phases).reshape(2, 1, 32, NX)
 
 
 def solution(mesh):

time: 54.6 us -> 54.2 us (level)
  local copies, waits for them, and re-layouts: 0.76 us -> 0.05 us
    unnamed x16, local copies, waits for them, and re-layouts: 0.69 us -> 0.05 us
  transfers between devices with their start and end apart: 1 -> 1, of which waited for: 1 -> 1; matrix products, arithmetic and copies ran while one was open for 0% -> 0% of each run, Pallas kernels for 0% -> 1%
where the time goes in v3:
time: 54.2 us; the launch traced here: 54 us
  blocking collectives  30.7 us (57%)
  waiting for transfers between devices  11.2 us (21%)
  starting transfers between devices  7.62 us (14%)
  Pallas kernels  4.35 us (8%)
    all_to_all x1, blocking collectives, per_device(): lax.all_to_all(mixed.reshape(256, 4, 128), ('tm', 'row'), split_axis=0, c...  30.7 us
    all_to_all x1, waiting for transfers between devices, per_device(): lax.all_to_all(mine, 'tm', split_axis=0, concat_axis=0, tiled=True)  11.2 us
    all_to_all x1, starting transfers between devices, per_device(): lax.all_to_all(mine, 'tm', split_axis=0, concat_axis=0, tiled=True)  7.62 us
    pallas_call x1, Pallas kernels, time_part(): pl.pallas_call(time_kernel, out_shape=jax.ShapeDtypeStruct((1024, 128), F...  2.59 us
    pallas_call x1, Pallas kernels, cross_part(): pl.pallas_call(cross_kernel, out_shape=jax.ShapeDtypeStruct((2, 32, NX),...  1.28 us
  transfers between devices with their start and end apart: 1, of which 1 were waited for; matrix products, arithmetic and copies ran while one was open for 0% of the time, Pallas kernels for 1%

profile of v3, /device:TPU:1, one launch (start us, length us, event | category | flops | bytes accessed | tf_op | source)
XLA Modules:
  0.0 54.0 jit_solution(17547801363746031532)
XLA Ops:
  0.0 0.0 copy-start.7
  0.0 0.0 copy-start.1
  0.0 0.0 copy-start.2
  0.0 0.0 copy-start.3
  0.0 0.0 copy-start.4
  0.0 0.0 copy-start.5
  0.0 7.6 %all-to-all-start = ((f32[8,16,8,128]{3,2,1,0:T(8,128)}), f32[8,16,8,128]{3,2,1,0:T(8,128)S(1)}, u32[]{:S(2)}, u32[]{:S(2)}) async-start(f32[8,16,8,128]{3,2,1,0:T(8,128)} %bitcast.12), calls=%async_computation | async-start | bytes 1048576 | tf_op jit(solution)/shard_map/all_to_all | solution.py:329
  7.7 0.0 copy-done.7
  7.7 0.5 prepare.1
  8.2 11.2 %all-to-all-done = f32[8,16,8,128]{3,2,1,0:T(8,128)S(1)} async-done(((f32[8,16,8,128]{3,2,1,0:T(8,128)}), f32[8,16,8,128]{3,2,1,0:T(8,128)S(1)}, u32[]{:S(2)}, u32[]{:S(2)}) %all-to-all-start) | async-done | bytes 524320 | tf_op jit(solution)/shard_map/all_to_all | solution.py:329
  19.4 0.0 copy-done.1
  19.4 0.0 copy-done.2
  19.4 0.0 copy-done.3
  19.4 0.0 copy-done.4
  19.4 0.0 copy-done.5
  19.4 2.6 %time_spectra.1 = f32[1024,128]{1,0:T(8,128)S(1)} custom-call(f32[8,128]{1,0:T(8,128)S(1)} %get-tuple-element.7.strength_ref, f32[1024,128]{1,0:T(8,128)S(1)} %bitcast.10, bf16[256,384]{1,0:T(8,128)(2,1)S(1)} %copy-done.1, f32[2,128,128]{2,1,0:T(8,128)S(1)} %copy-done.4, bf16[256,256]{1,0:T(8,128)(2,1)S(1)} %copy-done.3, bf16[256,256]{1,0:T(8,128)(2,1)S(1)} %copy-done.2, ...), custom_call_target="tpu_custom_call" | custom-call | tf_op jit(solution)/shard_map/time_spectra/pallas_call | solution.py:299
  22.0 0.0 copy-start
  22.0 0.0 copy-start.6
  22.0 30.7 %all_to_all.10 = f32[256,4,128]{2,1,0:T(4,128)S(1)} all-to-all(f32[256,4,128]{2,1,0:T(4,128)S(1)} %bitcast.11), channel_id=1, replica_groups=mesh['tm'=8,'row'=32] {'tm','row'}, dimensions={0} | all-to-all | bytes 1048576 | tf_op jit(solution)/shard_map/all_to_all | solution.py:332
  52.7 0.0 copy-done
  52.7 0.0 copy-done.6
  52.7 1.3 %cross_spectra.1 = f32[2,32,2048]{2,1,0:T(8,128)} custom-call(f32[1024,128]{1,0:T(8,128)S(1)} %bitcast.9, f32[2,32,2048]{2,1,0:T(8,128)S(1)} %get-tuple-element.8.phase_ref, bf16[2,256,256]{2,1,0:T(8,128)(2,1)S(1)} %copy-done, f32[2,16,128]{2,1,0:T(8,128)S(1)} %copy-done.6), custom_call_target="tpu_custom_call" | custom-call | tf_op jit(solution)/shard_map/cross_spectra/pallas_call | solution.py:313
Async XLA Ops:
  0.0 7.7 %copy-start.7 = (f32[1,64]{1,0:T(1,128)S(1)}, f32[1,64]{1,0:T(1,128)}, u32[]{:S(2)}) copy-start(f32[1,64]{1,0:T(1,128)} %screen_ref.1) | copy-start | bytes 772
  0.0 19.4 %copy-start.1 = (bf16[256,384]{1,0:T(8,128)(2,1)S(1)}, bf16[256,384]{1,0:T(8,128)(2,1)}, u32[]{:S(2)}) copy-start(bf16[256,384]{1,0:T(8,128)(2,1)} %constant.14.clone.one_ref) | copy-start | bytes 589828
  0.0 19.4 %copy-start.2 = (bf16[256,256]{1,0:T(8,128)(2,1)S(1)}, bf16[256,256]{1,0:T(8,128)(2,1)}, u32[]{:S(2)}) copy-start(bf16[256,256]{1,0:T(8,128)(2,1)} %constant.17.clone.within_ref) | copy-start | bytes 393220
  0.0 19.4 %copy-start.3 = (bf16[256,256]{1,0:T(8,128)(2,1)S(1)}, bf16[256,256]{1,0:T(8,128)(2,1)}, u32[]{:S(2)}) copy-start(bf16[256,256]{1,0:T(8,128)(2,1)} %constant.16.clone.two_ref) | copy-start | bytes 393220
  0.0 19.4 %copy-start.4 = (f32[2,128,128]{2,1,0:T(8,128)S(1)}, f32[2,128,128]{2,1,0:T(8,128)}, u32[]{:S(2)}) copy-start(f32[2,128,128]{2,1,0:T(8,128)} %constant.15.clone.twist_ref) | copy-start | bytes 393220
  0.0 19.4 %copy-start.5 = (bf16[128,256]{1,0:T(8,128)(2,1)S(1)}, bf16[128,256]{1,0:T(8,128)(2,1)}, u32[]{:S(2)}) copy-start(bf16[128,256]{1,0:T(8,128)(2,1)} %constant.18.clone.earlier_ref) | copy-start | bytes 196612
  0.0 19.3 %all-to-all-start = ((f32[8,16,8,128]{3,2,1,0:T(8,128)}), f32[8,16,8,128]{3,2,1,0:T(8,128)S(1)}, u32[]{:S(2)}, u32[]{:S(2)}) async-start(f32[8,16,8,128]{3,2,1,0:T(8,128)} %bitcast.12), calls=%async_computation | async-start | bytes 1048576 | tf_op jit(solution)/shard_map/all_to_all | solution.py:329
  22.0 30.7 %copy-start = (bf16[2,256,256]{2,1,0:T(8,128)(2,1)S(1)}, bf16[2,256,256]{2,1,0:T(8,128)(2,1)}, u32[]{:S(2)}) copy-start(bf16[2,256,256]{2,1,0:T(8,128)(2,1)} %constant.19.clone.table_ref) | copy-start | bytes 786436
  22.0 30.7 %copy-start.6 = (f32[2,16,128]{2,1,0:T(8,128)S(1)}, f32[2,16,128]{2,1,0:T(8,128)}, u32[]{:S(2)}) copy-start(f32[2,16,128]{2,1,0:T(8,128)} %constant.20.clone.twist_ref) | copy-start | bytes 49156

commit v4 on v3

--- a/solution.py
+++ b/solution.py
@@ -35,20 +35,20 @@
 def time_tables():
     index = np.arange(128)
     cos_one, sin_one = turns(index, index, 128)
-    one_high, one_low = two_parts(np.concatenate([cos_one, -sin_one], 0))
-    one = np.concatenate([one_high, one_high, one_low], 1)
+    one_high, one_low = two_parts(np.concatenate([cos_one, -sin_one], 1))
+    one = np.concatenate([one_high, one_high, one_low], 0)
     cos_twist, sin_twist = turns(index, index, NT)
     twist = np.stack([cos_twist, sin_twist]).astype(np.float32)
     cos_two, sin_two = turns(np.arange(64), index, 128)
     scale = 1.0 / math.sqrt(NT)
-    two = np.block([[cos_two, sin_two], [-sin_two, cos_two]]) * scale
-    two_high, two_low = two_parts(two)
-    two = np.concatenate([two_high, two_low], 0)
-    within = (index[:, None] <= index[None, :]).astype(np.float64)
-    within = np.concatenate([within, np.ones((128, 128))], 1)
-    within = np.concatenate([within, within], 0).astype(ml_dtypes.bfloat16)
-    earlier = (index[None, :] < index[:, None]).astype(np.float64)
-    earlier = np.concatenate([earlier, earlier], 1).astype(ml_dtypes.bfloat16)
+    two = np.concatenate(
+        two_parts(np.block([[cos_two, sin_two], [-sin_two, cos_two]]) * scale), 0
+    )
+    within = (index[None, :] <= index[:, None]).astype(np.float64)
+    within = np.concatenate([within, np.ones((16, 128))], 0)
+    within = np.concatenate([within, within], 1).astype(ml_dtypes.bfloat16)
+    earlier = (index[:, None] < index[None, :]).astype(np.float64)
+    earlier = np.concatenate([earlier, earlier], 0).astype(ml_dtypes.bfloat16)
     return one, twist, two, within, earlier
 
 
@@ -74,11 +74,19 @@
     return jnp.dot(left, right, preferred_element_type=F32)
 
 
-def dot_nt(left, right):
-    return lax.dot_general(left, right, (((1,), (1,)), ((), ())), preferred_element_type=F32)
-
-
-PAIRS = 2
+def exchange_blocks(values):
+    lane = lax.broadcasted_iota(jnp.int32, values[0].shape, 1)
+    for width in (32, 64):
+        low = (lane & width) == 0
+        step = width // 32
+        result = [None] * 4
+        for n in range(4):
+            if n & step == 0:
+                first, second = values[n], values[n + step]
+                result[n] = jnp.where(low, first, pltpu.roll(second, width, 1))
+                result[n + step] = jnp.where(low, pltpu.roll(first, 128 - width, 1), second)
+        values = result
+    return values
 
 
 def time_kernel(
@@ -90,73 +98,71 @@
     within_ref,
     earlier_ref,
     out_ref,
+    turned_ref,
     high_ref,
     low_ref,
-    stack_ref,
 ):
     points = range(8)
+    cuts = [slice(p * 128, (p + 1) * 128) for p in points]
     fourths = []
     for p in points:
-        sample = x_ref[pl.ds(p, 128, stride=8), :]
+        sample = x_ref[pl.ds(p, 128, stride=8), :].T
+        turned_ref[cuts[p], :] = sample
         square = sample * sample
-        fourths.append(jnp.concatenate(split(square * square), 1))
-    sums = dot(jnp.concatenate(fourths, 0), within_ref[...])
-    totals = [jnp.concatenate(split(sums[p * 128 : (p + 1) * 128, 128:]), 0) for p in points]
-    before = dot(earlier_ref[...], jnp.concatenate(totals, 1))
-    for p in points:
-        cut = slice(p * 128, (p + 1) * 128)
-        sample = x_ref[pl.ds(p, 128, stride=8), :]
-        square = sample * sample
-        density = (sums[cut, :128] + before[:, cut]) * (ionize_rate / NT)
-        polarization = (kerr_coeff * square + strength_ref[p : p + 1, :]) * sample
-        current = density * sample
-        for s, signal in enumerate((sample, polarization, current)):
-            high, low = split(signal)
-            lanes = slice((p * 3 + s) * 128, (p * 3 + s + 1) * 128)
-            stack_ref[:128, lanes] = high
-            stack_ref[128:, lanes] = low
-    for pair in range(PAIRS):
-        width = 3072 // PAIRS
-        lanes = slice(pair * width, (pair + 1) * width)
-        first = dot(one_ref[:, :256], stack_ref[:, lanes]) + dot(
-            one_ref[:, 256:], stack_ref[:128, lanes]
-        )
-        for n in range(width // 128):
-            p, s = divmod(pair * (width // 128) + n, 3)
-            re = first[:128, n * 128 : (n + 1) * 128]
-            im = first[128:, n * 128 : (n + 1) * 128]
+        fourths.append(jnp.concatenate(split(square * square), 0))
+    sums = dot(within_ref[...], jnp.concatenate(fourths, 1))
+    totals = [jnp.concatenate(split(sums[128:, cut]), 1) for cut in cuts]
+    before = dot(jnp.concatenate(totals, 0), earlier_ref[...])
+    for group in range(8 // GROUP):
+        rows = []
+        for p in range(group * GROUP, (group + 1) * GROUP):
+            sample = turned_ref[cuts[p], :]
+            density = (sums[:128, cuts[p]] + before[p * 16 : p * 16 + 1]) * (ionize_rate / NT)
+            polarization = (kerr_coeff * sample * sample + strength_ref[p : p + 1, :]) * sample
+            current = density * sample
+            for signal in (sample, polarization, current):
+                rows.append(jnp.concatenate(split(signal), 1))
+        rows = jnp.concatenate(rows, 0)
+        first = dot(rows, one_ref[:256]) + dot(rows[:, :128], one_ref[256:])
+        for n in range(GROUP * 3):
+            p, s = divmod(group * GROUP * 3 + n, 3)
+            re = first[n * 128 : (n + 1) * 128, :128]
+            im = first[n * 128 : (n + 1) * 128, 128:]
             cos_twist = twist_ref[0]
             sin_twist = twist_ref[1]
-            turned = jnp.concatenate(
-                [re * cos_twist + im * sin_twist, im * cos_twist - re * sin_twist], 1
-            )
-            high, low = split(turned)
-            for c in range(4):
-                rows = pl.ds((c * 8 + p) * 32, 32)
-                high_ref[s, rows, :] = high[c * 32 : (c + 1) * 32]
-                low_ref[s, rows, :] = low[c * 32 : (c + 1) * 32]
+            lanes = slice((s * 8 + p) * 128, (s * 8 + p + 1) * 128)
+            for part, value in enumerate(
+                (re * cos_twist + im * sin_twist, im * cos_twist - re * sin_twist)
+            ):
+                high, low = split(value)
+                high_ref[part * 128 : (part + 1) * 128, lanes] = high
+                low_ref[part * 128 : (part + 1) * 128, lanes] = low
     k2 = lax.broadcasted_iota(jnp.int32, (64, 128), 0)
     lane = lax.broadcasted_iota(jnp.int32, (64, 128), 1)
-    for c in range(4):
-        rows = pl.ds(c * 256, 256)
-        parts = []
-        for s in range(3):
-            both = dot_nt(two_ref[...], high_ref[s, rows, :])
-            rest = dot_nt(two_ref[:128], low_ref[s, rows, :])
-            value = both[:128] + both[128:] + rest
-            parts.append((value[:64], value[64:]))
-        scaled = (k2 * 128 + c * 32 + lane % 32).astype(F32) / NF
-        kerr = 0.2 * scaled
-        plasma = 0.5 / (1.0 + 64.0 * scaled * scaled)
-        for h in range(2):
-            cut = slice(h * 128, (h + 1) * 128)
-            (base_re, base_im), (kerr_re, kerr_im), (plasma_re, plasma_im) = [
-                (re[:, cut], im[:, cut]) for re, im in parts
-            ]
-            mixed_re = base_re - kerr * kerr_im - plasma * plasma_re
-            mixed_im = base_im + kerr * kerr_re - plasma * plasma_im
-            out_ref[pl.ds(c * 4 + h, 64, stride=16), :] = mixed_re
-            out_ref[pl.ds(c * 4 + 2 + h, 64, stride=16), :] = mixed_im
+    scaled = (k2 * 128 + lane).astype(F32) / NF
+    kerr = 0.2 * scaled
+    plasma = 0.5 / (1.0 + 64.0 * scaled * scaled)
+    for h in range(2):
+        mixed = [[], []]
+        for pair in range(2):
+            parts = []
+            for s in range(3):
+                lanes = slice((s * 8 + h * 4 + pair * 2) * 128, (s * 8 + h * 4 + pair * 2 + 2) * 128)
+                both = dot(two_ref[...], high_ref[:, lanes])
+                rest = dot(two_ref[:128], low_ref[:, lanes])
+                parts.append(both[:128] + both[128:] + rest)
+            for n in range(2):
+                (base_re, base_im), (kerr_re, kerr_im), (plasma_re, plasma_im) = [
+                    (part[:64, cuts[n]], part[64:, cuts[n]]) for part in parts
+                ]
+                mixed[0].append(base_re - kerr * kerr_im - plasma * plasma_re)
+                mixed[1].append(base_im + kerr * kerr_re - plasma * plasma_im)
+        for part in range(2):
+            for c, value in enumerate(exchange_blocks(mixed[part])):
+                out_ref[pl.ds(c * 4 + part * 2 + h, 64, stride=16), :] = value
+
+
+GROUP = 1
 
 
 def fft4(values):
@@ -301,7 +307,7 @@
         out_shape=jax.ShapeDtypeStruct((1024, 128), F32),
         in_specs=[in_vmem] * 7,
         out_specs=in_vmem,
-        scratch_shapes=[pltpu.VMEM((3, 1024, 256), BF16)] * 2 + [pltpu.VMEM((256, 3072), BF16)],
+        scratch_shapes=[pltpu.VMEM((1024, 128), F32)] + [pltpu.VMEM((256, 3072), BF16)] * 2,
         compiler_params=pltpu.CompilerParams(vmem_limit_bytes=32 * 2**20),
         name="time_spectra",
     )(strength, samples, *tables)

time: 54.2 us -> 54.1 us (level)
  no operation moved by 1% of the time
where the time goes in v4:
time: 54.1 us; the launch traced here: 53.9 us
  blocking collectives  30.7 us (57%)
  waiting for transfers between devices  11.2 us (21%)
  starting transfers between devices  7.62 us (14%)
  Pallas kernels  4.2 us (8%)
    all_to_all x1, blocking collectives, per_device(): lax.all_to_all(mixed.reshape(256, 4, 128), ('tm', 'row'), split_axis=0, c...  30.7 us
    all_to_all x1, waiting for transfers between devices, per_device(): lax.all_to_all(mine, 'tm', split_axis=0, concat_axis=0, tiled=True)  11.2 us
    all_to_all x1, starting transfers between devices, per_device(): lax.all_to_all(mine, 'tm', split_axis=0, concat_axis=0, tiled=True)  7.62 us
    pallas_call x1, Pallas kernels, time_part(): pl.pallas_call(time_kernel, out_shape=jax.ShapeDtypeStruct((1024, 128), F...  2.44 us
    pallas_call x1, Pallas kernels, cross_part(): pl.pallas_call(cross_kernel, out_shape=jax.ShapeDtypeStruct((2, 32, NX),...  1.28 us
  transfers between devices with their start and end apart: 1, of which 1 were waited for; matrix products, arithmetic and copies ran while one was open for 0% of the time, Pallas kernels for 1%

profile of v4, /device:TPU:1, one launch (start us, length us, event | category | flops | bytes accessed | tf_op | source)
XLA Modules:
  0.0 53.9 jit_solution(1621494549573009674)
XLA Ops:
  0.0 0.0 copy-start.7
  0.0 0.0 copy-start.1
  0.0 0.0 copy-start.2
  0.0 0.0 copy-start.3
  0.0 0.0 copy-start.4
  0.0 0.0 copy-start.5
  0.0 7.6 %all-to-all-start = ((f32[8,16,8,128]{3,2,1,0:T(8,128)}), f32[8,16,8,128]{3,2,1,0:T(8,128)S(1)}, u32[]{:S(2)}, u32[]{:S(2)}) async-start(f32[8,16,8,128]{3,2,1,0:T(8,128)} %bitcast.12), calls=%async_computation | async-start | bytes 1048576 | tf_op jit(solution)/shard_map/all_to_all | solution.py:335
  7.7 0.0 copy-done.7
  7.7 0.5 prepare.1
  8.2 11.2 %all-to-all-done = f32[8,16,8,128]{3,2,1,0:T(8,128)S(1)} async-done(((f32[8,16,8,128]{3,2,1,0:T(8,128)}), f32[8,16,8,128]{3,2,1,0:T(8,128)S(1)}, u32[]{:S(2)}, u32[]{:S(2)}) %all-to-all-start) | async-done | bytes 524320 | tf_op jit(solution)/shard_map/all_to_all | solution.py:335
  19.4 0.0 copy-done.1
  19.4 0.0 copy-done.2
  19.4 0.0 copy-done.3
  19.4 0.0 copy-done.4
  19.4 0.0 copy-done.5
  19.4 2.4 %time_spectra.1 = f32[1024,128]{1,0:T(8,128)S(1)} custom-call(f32[8,128]{1,0:T(8,128)S(1)} %get-tuple-element.7.strength_ref, f32[1024,128]{1,0:T(8,128)S(1)} %bitcast.9, bf16[384,256]{1,0:T(8,128)(2,1)S(1)} %copy-done.1, f32[2,128,128]{2,1,0:T(8,128)S(1)} %copy-done.3, bf16[256,256]{1,0:T(8,128)(2,1)S(1)} %copy-done.2, bf16[144,256]{1,0:T(8,128)(2,1)S(1)} %copy-done.4, ...), custom_call_target="tpu_custom_call" | custom-call | tf_op jit(solution)/shard_map/time_spectra/pallas_call | solution.py:305
  21.8 0.0 copy-start
  21.9 0.0 copy-start.6
  21.9 30.7 %all_to_all.10 = f32[256,4,128]{2,1,0:T(4,128)S(1)} all-to-all(f32[256,4,128]{2,1,0:T(4,128)S(1)} %bitcast.10), channel_id=1, replica_groups=mesh['tm'=8,'row'=32] {'tm','row'}, dimensions={0} | all-to-all | bytes 1048576 | tf_op jit(solution)/shard_map/all_to_all | solution.py:338
  52.6 0.0 copy-done
  52.6 0.0 copy-done.6
  52.6 1.3 %cross_spectra.1 = f32[2,32,2048]{2,1,0:T(8,128)} custom-call(f32[1024,128]{1,0:T(8,128)S(1)} %bitcast.11, f32[2,32,2048]{2,1,0:T(8,128)S(1)} %get-tuple-element.8.phase_ref, bf16[2,256,256]{2,1,0:T(8,128)(2,1)S(1)} %copy-done, f32[2,16,128]{2,1,0:T(8,128)S(1)} %copy-done.6), custom_call_target="tpu_custom_call" | custom-call | tf_op jit(solution)/shard_map/cross_spectra/pallas_call | solution.py:319
Async XLA Ops:
  0.0 7.7 %copy-start.7 = (f32[1,64]{1,0:T(1,128)S(1)}, f32[1,64]{1,0:T(1,128)}, u32[]{:S(2)}) copy-start(f32[1,64]{1,0:T(1,128)} %screen_ref.1) | copy-start | bytes 772
  0.0 19.4 %copy-start.1 = (bf16[384,256]{1,0:T(8,128)(2,1)S(1)}, bf16[384,256]{1,0:T(8,128)(2,1)}, u32[]{:S(2)}) copy-start(bf16[384,256]{1,0:T(8,128)(2,1)} %constant.14.clone.one_ref) | copy-start | bytes 589828
  0.0 19.4 %copy-start.2 = (bf16[256,256]{1,0:T(8,128)(2,1)S(1)}, bf16[256,256]{1,0:T(8,128)(2,1)}, u32[]{:S(2)}) copy-start(bf16[256,256]{1,0:T(8,128)(2,1)} %constant.16.clone.two_ref) | copy-start | bytes 393220
  0.0 19.4 %copy-start.3 = (f32[2,128,128]{2,1,0:T(8,128)S(1)}, f32[2,128,128]{2,1,0:T(8,128)}, u32[]{:S(2)}) copy-start(f32[2,128,128]{2,1,0:T(8,128)} %constant.15.clone.twist_ref) | copy-start | bytes 393220
  0.0 19.4 %copy-start.4 = (bf16[144,256]{1,0:T(8,128)(2,1)S(1)}, bf16[144,256]{1,0:T(8,128)(2,1)}, u32[]{:S(2)}) copy-start(bf16[144,256]{1,0:T(8,128)(2,1)} %constant.17.clone.within_ref) | copy-start | bytes 221188
  0.0 19.4 %copy-start.5 = (bf16[256,128]{1,0:T(8,128)(2,1)S(1)}, bf16[256,128]{1,0:T(8,128)(2,1)}, u32[]{:S(2)}) copy-start(bf16[256,128]{1,0:T(8,128)(2,1)} %constant.18.clone.earlier_ref) | copy-start | bytes 196612
  0.0 19.3 %all-to-all-start = ((f32[8,16,8,128]{3,2,1,0:T(8,128)}), f32[8,16,8,128]{3,2,1,0:T(8,128)S(1)}, u32[]{:S(2)}, u32[]{:S(2)}) async-start(f32[8,16,8,128]{3,2,1,0:T(8,128)} %bitcast.12), calls=%async_computation | async-start | bytes 1048576 | tf_op jit(solution)/shard_map/all_to_all | solution.py:335
  21.8 30.7 %copy-start = (bf16[2,256,256]{2,1,0:T(8,128)(2,1)S(1)}, bf16[2,256,256]{2,1,0:T(8,128)(2,1)}, u32[]{:S(2)}) copy-start(bf16[2,256,256]{2,1,0:T(8,128)(2,1)} %constant.19.clone.table_ref) | copy-start | bytes 786436
  21.9 30.7 %copy-start.6 = (f32[2,16,128]{2,1,0:T(8,128)S(1)}, f32[2,16,128]{2,1,0:T(8,128)}, u32[]{:S(2)}) copy-start(f32[2,16,128]{2,1,0:T(8,128)} %constant.20.clone.twist_ref) | copy-start | bytes 49156

commit v5 on v4

--- a/solution.py
+++ b/solution.py
@@ -20,6 +20,16 @@
 BF16 = jnp.bfloat16
 
 
+def places():
+    place = np.arange(256)
+    return place // 32, place // 8 % 4, place // 4 % 2, place // 2 % 2, place % 2
+
+
+def device_at():
+    z, x, y_hi, y_lo, core = places()
+    return ((y_hi * 4 + x) * 2 + y_lo) * 16 + z * 2 + core
+
+
 def two_parts(table):
     high = table.astype(ml_dtypes.bfloat16)
     low = (table - high.astype(np.float64)).astype(ml_dtypes.bfloat16)
@@ -39,7 +49,7 @@
     one = np.concatenate([one_high, one_high, one_low], 0)
     cos_twist, sin_twist = turns(index, index, NT)
     twist = np.stack([cos_twist, sin_twist]).astype(np.float32)
-    cos_two, sin_two = turns(np.arange(64), index, 128)
+    cos_two, sin_two = turns(device_at().reshape(4, 2, 16, 2)[:, 0, :, 0].ravel() // 4, index, 128)
     scale = 1.0 / math.sqrt(NT)
     two = np.concatenate(
         two_parts(np.block([[cos_two, sin_two], [-sin_two, cos_two]]) * scale), 0
@@ -53,8 +63,8 @@
 
 
 def cross_tables():
-    order = np.arange(128)
-    x_hi = (order % 32) * 4 + order // 32
+    even = device_at()[places()[1] % 2 == 0]
+    x_hi = (even % 32) * 4 + even // 64
     cos_one, sin_one = turns(x_hi, np.arange(128), 128)
     scale = 1.0 / math.sqrt(NX)
     table = np.block([[cos_one, -sin_one], [sin_one, cos_one]]) * scale
@@ -137,7 +147,8 @@
                 high, low = split(value)
                 high_ref[part * 128 : (part + 1) * 128, lanes] = high
                 low_ref[part * 128 : (part + 1) * 128, lanes] = low
-    k2 = lax.broadcasted_iota(jnp.int32, (64, 128), 0)
+    n = lax.broadcasted_iota(jnp.int32, (64, 128), 0)
+    k2 = (n // 2 % 2) * 32 + (n // 4 % 4) * 8 + (n % 2) * 4 + n // 16
     lane = lax.broadcasted_iota(jnp.int32, (64, 128), 1)
     scaled = (k2 * 128 + lane).astype(F32) / NF
     kerr = 0.2 * scaled
@@ -159,7 +170,9 @@
                 mixed[1].append(base_im + kerr * kerr_re - plasma * plasma_im)
         for part in range(2):
             for c, value in enumerate(exchange_blocks(mixed[part])):
-                out_ref[pl.ds(c * 4 + part * 2 + h, 64, stride=16), :] = value
+                for z in range(4):
+                    start = z * 256 + c // 2 * 128 + c % 2 * 4 + part * 2 + h
+                    out_ref[pl.ds(start, 16, stride=8), :] = value[z * 16 : z * 16 + 16]
 
 
 GROUP = 1
@@ -247,7 +260,7 @@
             for h in range(2):
                 j = part * 2 + h
                 pieces = [
-                    x_ref[pl.ds((2 * pair + odd) * 128 + j, 32, stride=4), :] for pair in range(4)
+                    x_ref[pl.ds((2 * pair + odd) * 32 + j, 8, stride=4), :] for pair in range(16)
                 ]
                 blocks.append(jnp.concatenate(pieces, 0).T)
     copies = []
@@ -336,7 +349,12 @@
     strength, phases = prepare_part(screen)
     mixed = time_part(strength, samples.reshape(1024, 128))
     blocks = lax.all_to_all(
-        mixed.reshape(256, 4, 128), ("tm", "row"), split_axis=0, concat_axis=0, tiled=True
+        mixed.reshape(256, 4, 128),
+        ("tm", "row"),
+        split_axis=0,
+        concat_axis=0,
+        axis_index_groups=[device_at().tolist()],
+        tiled=True,
     )
     return cross_part(blocks.reshape(1024, 128), phases).reshape(2, 1, 32, NX)
 

time: 54.1 us -> 53.9 us (level)
  no operation moved by 1% of the time
where the time goes in v5:
time: 53.9 us; the launch traced here: 53.7 us
  blocking collectives  30.6 us (57%)
  waiting for transfers between devices  11.2 us (21%)
  starting transfers between devices  7.62 us (14%)
  Pallas kernels  4.17 us (8%)
    all_to_all x1, blocking collectives, per_device(): lax.all_to_all(mixed.reshape(256, 4, 128), ('tm', 'row'), split_axis=0, c...  30.6 us
    all_to_all x1, waiting for transfers between devices, per_device(): lax.all_to_all(mine, 'tm', split_axis=0, concat_axis=0, tiled=True)  11.2 us
    all_to_all x1, starting transfers between devices, per_device(): lax.all_to_all(mine, 'tm', split_axis=0, concat_axis=0, tiled=True)  7.62 us
    pallas_call x1, Pallas kernels, time_part(): pl.pallas_call(time_kernel, out_shape=jax.ShapeDtypeStruct((1024, 128), F...  2.41 us
    pallas_call x1, Pallas kernels, cross_part(): pl.pallas_call(cross_kernel, out_shape=jax.ShapeDtypeStruct((2, 32, NX),...  1.28 us
  transfers between devices with their start and end apart: 1, of which 1 were waited for; matrix products, arithmetic and copies ran while one was open for 0% of the time, Pallas kernels for 1%

profile of v5, /device:TPU:1, one launch (start us, length us, event | category | flops | bytes accessed | tf_op | source)
XLA Modules:
  0.0 53.7 jit_solution(11003196387327512771)
XLA Ops:
  0.0 0.0 copy-start.7
  0.0 0.0 copy-start.1
  0.0 0.0 copy-start.2
  0.0 0.0 copy-start.3
  0.0 0.0 copy-start.4
  0.0 0.0 copy-start.5
  0.0 7.6 %all-to-all-start = ((f32[8,16,8,128]{3,2,1,0:T(8,128)}), f32[8,16,8,128]{3,2,1,0:T(8,128)S(1)}, u32[]{:S(2)}, u32[]{:S(2)}) async-start(f32[8,16,8,128]{3,2,1,0:T(8,128)} %bitcast.12), calls=%async_computation | async-start | bytes 1048576 | tf_op jit(solution)/shard_map/all_to_all | solution.py:348
  7.7 0.0 copy-done.7
  7.7 0.5 prepare.1
  8.2 11.2 %all-to-all-done = f32[8,16,8,128]{3,2,1,0:T(8,128)S(1)} async-done(((f32[8,16,8,128]{3,2,1,0:T(8,128)}), f32[8,16,8,128]{3,2,1,0:T(8,128)S(1)}, u32[]{:S(2)}, u32[]{:S(2)}) %all-to-all-start) | async-done | bytes 524320 | tf_op jit(solution)/shard_map/all_to_all | solution.py:348
  19.4 0.0 copy-done.1
  19.4 0.0 copy-done.2
  19.4 0.0 copy-done.3
  19.4 0.0 copy-done.4
  19.4 0.0 copy-done.5
  19.4 2.4 %time_spectra.1 = f32[1024,128]{1,0:T(8,128)S(1)} custom-call(f32[8,128]{1,0:T(8,128)S(1)} %get-tuple-element.7.strength_ref, f32[1024,128]{1,0:T(8,128)S(1)} %bitcast.9, bf16[384,256]{1,0:T(8,128)(2,1)S(1)} %copy-done.1, f32[2,128,128]{2,1,0:T(8,128)S(1)} %copy-done.3, bf16[256,256]{1,0:T(8,128)(2,1)S(1)} %copy-done.2, bf16[144,256]{1,0:T(8,128)(2,1)S(1)} %copy-done.4, ...), custom_call_target="tpu_custom_call" | custom-call | tf_op jit(solution)/shard_map/time_spectra/pallas_call | solution.py:318
  21.8 0.0 copy-start
  21.8 0.0 copy-start.6
  21.8 30.6 %all_to_all.10 = f32[256,4,128]{2,1,0:T(4,128)S(1)} all-to-all(f32[256,4,128]{2,1,0:T(4,128)S(1)} %bitcast.10), channel_id=1, replica_groups={{0,1,16,17,128,129,144,145,32,33,48,49,160,161,176,177,64,65,80,81,192,..., dimensions={0} | all-to-all | bytes 1048576 | tf_op jit(solution)/shard_map/all_to_all | solution.py:351
  52.4 0.0 copy-done
  52.4 0.0 copy-done.6
  52.4 1.3 %cross_spectra.1 = f32[2,32,2048]{2,1,0:T(8,128)} custom-call(f32[1024,128]{1,0:T(8,128)S(1)} %bitcast.11, f32[2,32,2048]{2,1,0:T(8,128)S(1)} %get-tuple-element.8.phase_ref, bf16[2,256,256]{2,1,0:T(8,128)(2,1)S(1)} %copy-done, f32[2,16,128]{2,1,0:T(8,128)S(1)} %copy-done.6), custom_call_target="tpu_custom_call" | custom-call | tf_op jit(solution)/shard_map/cross_spectra/pallas_call | solution.py:332
Async XLA Ops:
  0.0 7.7 %copy-start.7 = (f32[1,64]{1,0:T(1,128)S(1)}, f32[1,64]{1,0:T(1,128)}, u32[]{:S(2)}) copy-start(f32[1,64]{1,0:T(1,128)} %screen_ref.1) | copy-start | bytes 772
  0.0 19.4 %copy-start.1 = (bf16[384,256]{1,0:T(8,128)(2,1)S(1)}, bf16[384,256]{1,0:T(8,128)(2,1)}, u32[]{:S(2)}) copy-start(bf16[384,256]{1,0:T(8,128)(2,1)} %constant.14.clone.one_ref) | copy-start | bytes 589828
  0.0 19.4 %copy-start.2 = (bf16[256,256]{1,0:T(8,128)(2,1)S(1)}, bf16[256,256]{1,0:T(8,128)(2,1)}, u32[]{:S(2)}) copy-start(bf16[256,256]{1,0:T(8,128)(2,1)} %constant.16.clone.two_ref) | copy-start | bytes 393220
  0.0 19.4 %copy-start.3 = (f32[2,128,128]{2,1,0:T(8,128)S(1)}, f32[2,128,128]{2,1,0:T(8,128)}, u32[]{:S(2)}) copy-start(f32[2,128,128]{2,1,0:T(8,128)} %constant.15.clone.twist_ref) | copy-start | bytes 393220
  0.0 19.4 %copy-start.4 = (bf16[144,256]{1,0:T(8,128)(2,1)S(1)}, bf16[144,256]{1,0:T(8,128)(2,1)}, u32[]{:S(2)}) copy-start(bf16[144,256]{1,0:T(8,128)(2,1)} %constant.17.clone.within_ref) | copy-start | bytes 221188
  0.0 19.4 %copy-start.5 = (bf16[256,128]{1,0:T(8,128)(2,1)S(1)}, bf16[256,128]{1,0:T(8,128)(2,1)}, u32[]{:S(2)}) copy-start(bf16[256,128]{1,0:T(8,128)(2,1)} %constant.18.clone.earlier_ref) | copy-start | bytes 196612
  0.0 19.3 %all-to-all-start = ((f32[8,16,8,128]{3,2,1,0:T(8,128)}), f32[8,16,8,128]{3,2,1,0:T(8,128)S(1)}, u32[]{:S(2)}, u32[]{:S(2)}) async-start(f32[8,16,8,128]{3,2,1,0:T(8,128)} %bitcast.12), calls=%async_computation | async-start | bytes 1048576 | tf_op jit(solution)/shard_map/all_to_all | solution.py:348
  21.8 30.6 %copy-start = (bf16[2,256,256]{2,1,0:T(8,128)(2,1)S(1)}, bf16[2,256,256]{2,1,0:T(8,128)(2,1)}, u32[]{:S(2)}) copy-start(bf16[2,256,256]{2,1,0:T(8,128)(2,1)} %constant.19.clone.table_ref) | copy-start | bytes 786436
  21.8 30.6 %copy-start.6 = (f32[2,16,128]{2,1,0:T(8,128)S(1)}, f32[2,16,128]{2,1,0:T(8,128)}, u32[]{:S(2)}) copy-start(f32[2,16,128]{2,1,0:T(8,128)} %constant.20.clone.twist_ref) | copy-start | bytes 49156
